TPU v7x, 32 devices: a whole 2x2x4 slice. The times are simulated.
32 devices in a mesh: sec: 2 (over x), lat: 4 (over z), lon: 4 (over y, core).
Axes of the slice: x: 2, y: 2, z: 4, core: 2. Of those that a mesh axis runs over, the one named last changes fastest.
Arguments:
- spectra: float32 [36, 36, 32, 512], P('sec', None, 'lat', 'lon'), may hold values from 0 to 2
- currents: float32 [2, 8, 32, 512], P(None, 'sec', 'lat', 'lon'), may hold values from -3 to 3
- land_mask: int32 [32, 512], P('lat', 'lon'), may hold values 0 or 1
- diffusion: float32 [32, 512], P('lat', 'lon'), may hold values from 0.08 to 0.19
- courant: float32 [36], P('sec'), may hold values from 0.15 to 0.45
- stokes_weight: float32 [36], P('sec'), may hold values from 0.02 to 0.1
- stress_weight: float32 [36], P('sec'), may hold values from 0.02 to 0.1
Outputs:
- new_spectra: float32 [36, 36, 32, 512], P('sec', None, 'lat', 'lon')
- new_currents: float32 [2, 8, 32, 512], P(None, 'sec', 'lat', 'lon')
Inputs may be any that keep to these rules, and one draw needn't show every extreme that they name: `land_mask`: 1 marks a sea column, 0 a land column.
All inputs are finite; a program needn't handle non-finite values. No bound on the sum of `land_mask` on one device may be relied on, other than what follows from the above.
Results may differ from a plain program's by a relative error of at most 0.0001.
Values sent between devices are 32-bit elements; how exact they have to be, the bound alone decides.
No kernel may reach another device: no remote copies, remote signals or barrier semaphores. Data moves between devices by JAX's collectives and lax.ppermute only.
A program may use at most 128 MiB of HBM per device.

v0:
```python
import math

import jax
import jax.numpy as jnp
from jax import lax
from jax.sharding import PartitionSpec as P

ITERS = 4


current_gain = 0.1
stress_gain = 0.5


def broadcast(array, axis, root):
    mine = lax.axis_index(axis) == root
    return lax.psum(jnp.where(mine, array, jnp.zeros_like(array)), axis)


def passed_along(value, axis, steps):
    count = lax.axis_size(axis)
    pairs = [(source, (source + steps) % count) for source in range(count)]
    return lax.ppermute(value, axis, pairs)


def passed_along_2(value, axis, steps):
    count = lax.axis_size(axis)
    leading, last = (max(0, -steps), min(count, count - steps))
    return lax.ppermute(value, axis, [(source, source + steps) for source in range(leading, last)])


def padded(block, sides, width):
    for axis, dim in sides:
        count = lax.axis_size(axis)
        forward = [(i, i + 1) for i in range(count - 1)]
        forward.append((count - 1, 0))
        backward = [(target, source) for source, target in forward]
        low = lax.ppermute(
            lax.slice_in_dim(block, block.shape[dim] - width, None, axis=dim), axis, forward
        )
        high = lax.ppermute(lax.slice_in_dim(block, 0, width, axis=dim), axis, backward)
        block = jnp.concatenate([low, block, high], axis=dim)
    return block


def heading_tables(directions):
    heading = (jnp.arange(directions).astype(jnp.float32) + 0.5) * (2.0 * math.pi / directions)
    return (jnp.cos(heading), jnp.sin(heading))


def wave_update(
    energy,
    west_cell,
    east_cell,
    south_cell,
    north_cell,
    speed,
    cosine_table,
    sine_table,
    surface,
    sea_cells,
):
    speed_x = (speed[:, None] * cosine_table[None])[:, :, None, None]
    speed_y = (speed[:, None] * sine_table[None])[:, :, None, None]
    step_x = jnp.maximum(speed_x, 0.0) * (energy - west_cell) + jnp.minimum(speed_x, 0.0) * (
        east_cell - energy
    )
    step_y = jnp.maximum(speed_y, 0.0) * (energy - south_cell) + jnp.minimum(speed_y, 0.0) * (
        north_cell - energy
    )
    advected = energy - step_x - step_y
    doppler = 1.0 + current_gain * (
        surface[0][None] * cosine_table[:, None, None]
        + surface[1][None] * sine_table[:, None, None]
    )
    return sea_cells * (advected * doppler)


def coupling_weights(stokes_w, stress_w, cosine_table, sine_table):
    stacked = jnp.stack(
        [
            stokes_w[:, None] * cosine_table[None],
            stokes_w[:, None] * sine_table[None],
            stress_w[:, None] * cosine_table[None],
            stress_w[:, None] * sine_table[None],
        ]
    )
    return stacked.reshape(4, stokes_w.shape[0] * cosine_table.shape[0])


def vertical_rate(level):
    return 0.04 + 0.0125 * (7 * level % 5).astype(jnp.float32)


def coriolis_rate(row_index, total_rows):
    return 0.05 + 0.1 * (row_index.astype(jnp.float32) + 0.5) / total_rows


def valid_rows(first_row, row_count, total_rows):
    row_index = first_row + jnp.arange(row_count)
    return ((row_index >= 0) & (row_index < total_rows)).astype(jnp.float32)


def ocean_step(extended, column_data, first_level, first_row, total_levels, total_rows):
    center = extended[:, 1:-1, 1:-1, 1:-1]
    laplace = (
        extended[:, 1:-1, 2:, 1:-1]
        + extended[:, 1:-1, :-2, 1:-1]
        + extended[:, 1:-1, 1:-1, 2:]
        + extended[:, 1:-1, 1:-1, :-2]
        - 4.0 * center
    )
    level_above = extended[:, :-2, 1:-1, 1:-1]
    level_below = extended[:, 2:, 1:-1, 1:-1]
    level = first_level + 1 + jnp.arange(center.shape[1])
    has_up = (level > 0)[:, None, None]
    has_down = (level < total_levels - 1)[:, None, None]
    mixing = vertical_rate(level)[:, None, None]
    vertical = mixing * (
        jnp.where(has_up, level_above - center, 0.0)
        + jnp.where(has_down, level_below - center, 0.0)
    )
    stokes_decay = (1.0 / (1.0 + level.astype(jnp.float32)))[:, None, None]
    top_gain = jnp.where(level == 0, stress_gain, 0.0)[:, None, None]
    row_index = first_row + 1 + jnp.arange(center.shape[2])
    coriolis = coriolis_rate(row_index, total_rows)[:, None]
    sea_cells = column_data[0]
    kappa = column_data[1]
    zonal = center[0]
    meridional = center[1]
    zonal_new = sea_cells * (
        zonal
        + kappa * laplace[0]
        + vertical[0]
        + coriolis * (meridional + stokes_decay * column_data[3])
        + top_gain * column_data[4]
    )
    meridional_new = sea_cells * (
        meridional
        + kappa * laplace[1]
        + vertical[1]
        - coriolis * (zonal + stokes_decay * column_data[2])
        + top_gain * column_data[5]
    )
    return jnp.stack([zonal_new, meridional_new])


def shards(spectra, currents, land_mask, diffusion, courant, stokes_weight, stress_weight):
    freq_dev, directions, tile_rows, tile_cols = spectra.shape
    levels = currents.shape[1]
    sec_count = lax.axis_size("sec")
    lat_count = lax.axis_size("lat")
    sec_index = lax.axis_index("sec")
    lat_index = lax.axis_index("lat")
    total_rows = tile_rows * lat_count
    total_levels = levels * sec_count
    level_base = sec_index * levels
    row_base = lat_index * tile_rows
    sea_cells = land_mask.astype(jnp.float32)
    cosine_table, sine_table = heading_tables(directions)
    surface = broadcast(currents[:, 0], "sec", 0)
    quarter = directions // 4
    east_going = jnp.concatenate(
        [spectra[:, :quarter, :, -1], spectra[:, 3 * quarter :, :, -1]], axis=1
    )
    west_going = spectra[:, quarter : 3 * quarter, :, 0]
    north_going = spectra[:, : 2 * quarter, -1, :]
    south_going = spectra[:, 2 * quarter :, 0, :]
    got_west = passed_along(east_going, "lon", 1)
    got_east = passed_along(west_going, "lon", -1)
    got_south = passed_along_2(north_going, "lat", 1)
    got_north = passed_along_2(south_going, "lat", -1)
    zero_quarter = jnp.zeros((freq_dev, quarter, tile_rows), jnp.float32)
    zero_half = jnp.zeros((freq_dev, 2 * quarter, tile_rows), jnp.float32)
    zero_across = jnp.zeros((freq_dev, 2 * quarter, tile_cols), jnp.float32)
    west_rim = jnp.concatenate([got_west[:, :quarter], zero_half, got_west[:, quarter:]], axis=1)
    east_rim = jnp.concatenate([zero_quarter, got_east, zero_quarter], axis=1)
    south_rim = jnp.concatenate([got_south, zero_across], axis=1)
    north_rim = jnp.concatenate([zero_across, got_north], axis=1)
    west_cell = jnp.concatenate([west_rim[:, :, :, None], spectra[:, :, :, :-1]], axis=3)
    east_cell = jnp.concatenate([spectra[:, :, :, 1:], east_rim[:, :, :, None]], axis=3)
    south_cell = jnp.concatenate([south_rim[:, :, None], spectra[:, :, :-1]], axis=2)
    north_cell = jnp.concatenate([spectra[:, :, 1:], north_rim[:, :, None]], axis=2)
    new_spectra = wave_update(
        spectra,
        west_cell,
        east_cell,
        south_cell,
        north_cell,
        courant,
        cosine_table,
        sine_table,
        surface,
        sea_cells,
    )
    weights = coupling_weights(stokes_weight, stress_weight, cosine_table, sine_table)
    partial_value = jnp.dot(
        weights,
        new_spectra.reshape(freq_dev * directions, tile_rows * tile_cols),
        precision=lax.Precision.HIGHEST,
        preferred_element_type=jnp.float32,
    )
    coupling = lax.psum(partial_value, "sec").reshape(4, tile_rows, tile_cols)
    column_data = jnp.concatenate([sea_cells[None], diffusion[None], coupling], axis=0)
    fields = currents * sea_cells
    row_ok = valid_rows(row_base - 1, tile_rows + 2, total_rows)[:, None]
    for iteration in range(ITERS):
        extended = padded(fields, (("sec", 1), ("lat", 2), ("lon", 3)), 1)
        extended = extended * row_ok
        fields = ocean_step(
            extended, column_data, level_base - 1, row_base - 1, total_levels, total_rows
        )
    return (new_spectra, fields)


def solution(mesh):
    in_specs = (
        P("sec", None, "lat", "lon"),
        P(None, "sec", "lat", "lon"),
        P("lat", "lon"),
        P("lat", "lon"),
        P("sec"),
        P("sec"),
        P("sec"),
    )
    out_specs = (P("sec", None, "lat", "lon"), P(None, "sec", "lat", "lon"))
    return jax.shard_map(shards, mesh=mesh, in_specs=in_specs, out_specs=out_specs, check_vma=False)
```

profile of v0, /device:TPU:0, one launch (start us, length us, event | category | flops | bytes accessed | tf_op | source)
XLA Modules:
  0.0 131.1 jit_solution(11724753899061185363)
XLA Ops:
  0.6 2.7 %fusion.83 = (f32[18,9,8,1]{3,2,1,0:T(8,128)S(1)}, f32[18,9,8,1]{3,2,1,0:T(8,128)}) fusion(f32[18,36,8,128]{3,2,1,0:T(8,128)} %param.7), kind=kLoop, calls=%fused_computation.192 | loop fusion | bytes 20736 | tf_op jit(solution)/shard_map/slice | solution.py:164
  3.3 2.0 %copy.24 = f32[18,9,8,1]{1,2,0,3:T(8,128)S(1)} copy(f32[18,9,8,1]{3,2,1,0:T(8,128)} %get-tuple-element.9) | data formatting | bytes 10368
  8.6 2.9 %copy.25 = f32[18,18,8,1]{1,2,0,3:T(8,128)} copy(f32[18,18,8,1]{3,2,1,0:T(8,128)} %slice.312) | data formatting | bytes 20736
  11.5 2.0 %collective-permute-start.1 = (f32[18,18,8]{1,2,0:T(8,128)}, f32[18,18,8]{1,2,0:T(8,128)}, u32[]{:S(2)}, u32[]{:S(2)}) collective-permute-start(f32[18,18,8]{1,2,0:T(8,128)} %bitcast.3), channel_id=1, source_target_pairs={{0,3},{1,0},{2,1},{3,2},{4,7},{5,4},{6,5},{7,6},{8,11},{9,8},{10,9... | collective-permute-start | bytes 31112 | tf_op jit(solution)/shard_map/ppermute | solution.py:23
  13.7 4.3 %collective-permute-start.2 = (f32[18,18,128]{2,1,0:T(8,128)S(1)}, f32[18,18,128]{2,1,0:T(8,128)S(1)}, u32[]{:S(2)}, u32[]{:S(2)}) collective-permute-start(f32[18,18,128]{2,1,0:T(8,128)S(1)} %bitcast.39), channel_id=1, source_target_pairs={{0,4},{4,8},{8,12},{1,5},{5,9},{9,13},{2,6},{6,10},{10,14},{3,7},{... | collective-permute-start | bytes 497672 | tf_op jit(solution)/shard_map/ppermute | solution.py:29
  20.7 3.2 %fusion.82 = (f32[18,36,8,127]{3,2,1,0:T(8,128)}, f32[18,36,8,127]{3,2,1,0:T(8,128)}) fusion(f32[18,36,8,128]{3,2,1,0:T(8,128)S(1)} %copy-done), kind=kLoop, calls=%fused_computation.191 | loop fusion | bytes 10533888 | tf_op jit(solution)/shard_map/slice | solution.py:181
  23.9 3.0 %fusion.80 = (f32[18,36,7,128]{3,2,1,0:T(8,128)}, f32[18,36,7,128]{3,2,1,0:T(8,128)}) fusion(f32[18,36,8,128]{3,2,1,0:T(8,128)S(1)} %copy-done), kind=kLoop, calls=%fused_computation.189 | loop fusion | bytes 9289728 | tf_op jit(solution)/shard_map/slice | solution.py:183
  28.6 5.0 %psum.14 = f32[2,8,128]{2,1,0:T(8,128)S(1)} all-reduce(f32[2,8,128]{2,1,0:T(8,128)S(1)} %select_bitcast_fusion), channel_id=1, replica_groups=mesh['sec'=2,'lat'=4,'lon'=4] {'sec'}, use_global_device_ids=true, to_apply=%region_0.1 | all-reduce | flops 2048 | bytes 16384 | tf_op jit(solution)/shard_map/psum | solution.py:17
  43.2 5.4 %collective-permute-start.7 = (f32[2,6,1,128]{3,2,1,0:T(1,128)S(1)}, f32[2,6,1,128]{3,2,1,0:T(1,128)S(1)}, u32[]{:S(2)}, u32[]{:S(2)}) collective-permute-start(f32[2,6,1,128]{3,2,1,0:T(1,128)S(1)} %get-tuple-element.43), channel_id=1, source_target_pairs={{4,0},{8,4},{12,8},{0,12},{5,1},{9,5},{13,9},{1,13},{6,2},{10,6},{... | collective-permute-start | bytes 18440 | tf_op jit(solution)/shard_map/ppermute | solution.py:41
  50.0 4.0 %collective-permute-done.6 = f32[2,6,1,128]{3,2,1,0:T(1,128)S(1)} collective-permute-done((f32[2,6,1,128]{3,2,1,0:T(1,128)S(1)}, f32[2,6,1,128]{3,2,1,0:T(1,128)S(1)}, u32[]{:S(2)}, u32[]{:S(2)}) %collective-permute-start.6) | collective-permute-done | bytes 6176 | tf_op jit(solution)/shard_map/ppermute | solution.py:38
  56.3 2.6 %copy.16 = f32[18,36,8,1]{3,2,1,0:T(8,128)} copy(f32[18,36,8,1]{1,2,3,0:T(8,128)S(1)} %maximum_bitcast_fusion) | data formatting | bytes 41472 | tf_op jit(solution)/shard_map/broadcast_in_dim | solution.py:180
  58.9 2.7 %copy.18 = f32[18,36,8,1]{3,2,1,0:T(8,128)} copy(f32[18,36,8,1]{1,2,3,0:T(8,128)S(1)} %maximum_bitcast_fusion.1) | data formatting | bytes 41472 | tf_op jit(solution)/shard_map/broadcast_in_dim | solution.py:181
  65.6 6.6 %fusion.8 = f32[18,36,8,128]{3,2,1,0:T(8,128)S(1)} fusion(f32[18,36,8,128]{3,2,1,0:T(8,128)S(1)} %copy-done, f32[18,36,8,127]{3,2,1,0:T(8,128)} %get-tuple-element.7, f32[18,36,8,1]{3,2,1,0:T(8,128)} %copy.16, f32[18,36,8,1]{3,2,1,0:T(8,128)} %copy.18, f32[18,36,8,127]{3,2,1,0:T(8,128)S(1)} %copy-done.2, f32[18,36,7,128]{3,2,1,0:T(8,128)} %get-tuple-element.3, ...), kind=kLoop, calls=%fused_computation.9 | loop fusion | flops 11943936 | bytes 16087168 | tf_op jit(solution)/shard_map/mul | solution.py:76
  75.4 8.2 %psum.15 = f32[4,1024]{1,0:T(4,128)S(1)} all-reduce(f32[4,1024]{1,0:T(4,128)S(1)} %fusion), channel_id=1, replica_groups=mesh['sec'=2,'lat'=4,'lon'=4] {'sec'}, use_global_device_ids=true, to_apply=%region_1.2 | all-reduce | flops 4096 | bytes 32768 | tf_op jit(solution)/shard_map/psum | solution.py:203
  88.1 2.0 %collective-permute-start.12 = (f32[2,6,1,128]{3,2,1,0:T(1,128)S(1)}, f32[2,6,1,128]{3,2,1,0:T(1,128)S(1)}, u32[]{:S(2)}, u32[]{:S(2)}) collective-permute-start(f32[2,6,1,128]{3,2,1,0:T(1,128)S(1)} %get-tuple-element.40), channel_id=1, source_target_pairs={{0,4},{4,8},{8,12},{12,0},{1,5},{5,9},{9,13},{13,1},{2,6},{6,10},{... | collective-permute-start | bytes 18440 | tf_op jit(solution)/shard_map/ppermute | solution.py:38
  91.7 1.9 %collective-permute-done.12 = f32[2,6,1,128]{3,2,1,0:T(1,128)S(1)} collective-permute-done((f32[2,6,1,128]{3,2,1,0:T(1,128)S(1)}, f32[2,6,1,128]{3,2,1,0:T(1,128)S(1)}, u32[]{:S(2)}, u32[]{:S(2)}) %collective-permute-start.12) | collective-permute-done | bytes 6176 | tf_op jit(solution)/shard_map/ppermute | solution.py:38
  96.0 2.9 %collective-permute-done.14 = f32[2,6,10,1]{3,2,1,0:T(8,128)S(1)} collective-permute-done((f32[2,6,10,1]{3,2,1,0:T(8,128)S(1)}, f32[2,6,10,1]{3,2,1,0:T(8,128)S(1)}, u32[]{:S(2)}, u32[]{:S(2)}) %collective-permute-start.14) | collective-permute-done | bytes 512 | tf_op jit(solution)/shard_map/ppermute | solution.py:38
  104.7 2.0 %collective-permute-start.18 = (f32[2,6,1,128]{3,2,1,0:T(1,128)S(1)}, f32[2,6,1,128]{3,2,1,0:T(1,128)S(1)}, u32[]{:S(2)}, u32[]{:S(2)}) collective-permute-start(f32[2,6,1,128]{3,2,1,0:T(1,128)S(1)} %get-tuple-element.38), channel_id=1, source_target_pairs={{0,4},{4,8},{8,12},{12,0},{1,5},{5,9},{9,13},{13,1},{2,6},{6,10},{... | collective-permute-start | bytes 18440 | tf_op jit(solution)/shard_map/ppermute | solution.py:38
  108.3 1.9 %collective-permute-done.18 = f32[2,6,1,128]{3,2,1,0:T(1,128)S(1)} collective-permute-done((f32[2,6,1,128]{3,2,1,0:T(1,128)S(1)}, f32[2,6,1,128]{3,2,1,0:T(1,128)S(1)}, u32[]{:S(2)}, u32[]{:S(2)}) %collective-permute-start.18) | collective-permute-done | bytes 6176 | tf_op jit(solution)/shard_map/ppermute | solution.py:38
  110.8 2.7 %collective-permute-done.21 = f32[2,6,10,1]{3,2,1,0:T(8,128)S(1)} collective-permute-done((f32[2,6,10,1]{3,2,1,0:T(8,128)S(1)}, f32[2,6,10,1]{3,2,1,0:T(8,128)S(1)}, u32[]{:S(2)}, u32[]{:S(2)}) %collective-permute-start.21) | collective-permute-done | bytes 512 | tf_op jit(solution)/shard_map/ppermute | solution.py:41
  119.3 2.0 %collective-permute-start.24 = (f32[2,6,1,128]{3,2,1,0:T(1,128)S(1)}, f32[2,6,1,128]{3,2,1,0:T(1,128)S(1)}, u32[]{:S(2)}, u32[]{:S(2)}) collective-permute-start(f32[2,6,1,128]{3,2,1,0:T(1,128)S(1)} %get-tuple-element.36), channel_id=1, source_target_pairs={{0,4},{4,8},{8,12},{12,0},{1,5},{5,9},{9,13},{13,1},{2,6},{6,10},{... | collective-permute-start | bytes 18440 | tf_op jit(solution)/shard_map/ppermute | solution.py:38
  122.9 1.9 %collective-permute-done.24 = f32[2,6,1,128]{3,2,1,0:T(1,128)S(1)} collective-permute-done((f32[2,6,1,128]{3,2,1,0:T(1,128)S(1)}, f32[2,6,1,128]{3,2,1,0:T(1,128)S(1)}, u32[]{:S(2)}, u32[]{:S(2)}) %collective-permute-start.24) | collective-permute-done | bytes 6176 | tf_op jit(solution)/shard_map/ppermute | solution.py:38
  125.5 1.7 %collective-permute-done.27 = f32[2,6,10,1]{3,2,1,0:T(8,128)S(1)} collective-permute-done((f32[2,6,10,1]{3,2,1,0:T(8,128)S(1)}, f32[2,6,10,1]{3,2,1,0:T(8,128)S(1)}, u32[]{:S(2)}, u32[]{:S(2)}) %collective-permute-start.27) | collective-permute-done | bytes 512 | tf_op jit(solution)/shard_map/ppermute | solution.py:41
  127.2 2.9 %collective-permute-done.26 = f32[2,6,10,1]{3,2,1,0:T(8,128)S(1)} collective-permute-done((f32[2,6,10,1]{3,2,1,0:T(8,128)S(1)}, f32[2,6,10,1]{3,2,1,0:T(8,128)S(1)}, u32[]{:S(2)}, u32[]{:S(2)}) %collective-permute-start.26) | collective-permute-done | bytes 512 | tf_op jit(solution)/shard_map/ppermute | solution.py:38
  (172 shorter events, 53.4 us)
Async XLA Ops:
  7.0 41.5 %collective-permute-start = (f32[18,18,8]{1,2,0:T(8,128)}, f32[18,18,8]{1,2,0:T(8,128)S(1)}, u32[]{:S(2)}, u32[]{:S(2)}) collective-permute-start(f32[18,18,8]{1,2,0:T(8,128)} %pad_maximum_fusion.4), channel_id=1, source_target_pairs={{0,1},{1,2},{2,3},{3,0},{4,5},{5,6},{6,7},{7,4},{8,9},{9,10},{10,1... | collective-permute-start | bytes 31112 | tf_op jit(solution)/shard_map/ppermute | solution.py:23
  11.5 43.7 %collective-permute-start.1 = (f32[18,18,8]{1,2,0:T(8,128)}, f32[18,18,8]{1,2,0:T(8,128)}, u32[]{:S(2)}, u32[]{:S(2)}) collective-permute-start(f32[18,18,8]{1,2,0:T(8,128)} %bitcast.3), channel_id=1, source_target_pairs={{0,3},{1,0},{2,1},{3,2},{4,7},{5,4},{6,5},{7,6},{8,11},{9,8},{10,9... | collective-permute-start | bytes 31112 | tf_op jit(solution)/shard_map/ppermute | solution.py:23
  13.7 50.1 %collective-permute-start.2 = (f32[18,18,128]{2,1,0:T(8,128)S(1)}, f32[18,18,128]{2,1,0:T(8,128)S(1)}, u32[]{:S(2)}, u32[]{:S(2)}) collective-permute-start(f32[18,18,128]{2,1,0:T(8,128)S(1)} %bitcast.39), channel_id=1, source_target_pairs={{0,4},{4,8},{8,12},{1,5},{5,9},{9,13},{2,6},{6,10},{10,14},{3,7},{... | collective-permute-start | bytes 497672 | tf_op jit(solution)/shard_map/ppermute | solution.py:29
  18.6 23.2 %collective-permute-start.5 = (f32[2,1,8,128]{3,2,1,0:T(8,128)}, f32[2,1,8,128]{3,2,1,0:T(8,128)S(1)}, u32[]{:S(2)}, u32[]{:S(2)}) collective-permute-start(f32[2,1,8,128]{3,2,1,0:T(8,128)} %get-tuple-element.51), channel_id=1, source_target_pairs={{16,0},{0,16},{17,1},{1,17},{18,2},{2,18},{19,3},{3,19},{20,4},{4,... | collective-permute-start | bytes 24584 | tf_op jit(solution)/shard_map/ppermute | solution.py:41
  20.1 23.0 %collective-permute-start.4 = (f32[2,1,8,128]{3,2,1,0:T(8,128)}, f32[2,1,8,128]{3,2,1,0:T(8,128)S(1)}, u32[]{:S(2)}, u32[]{:S(2)}) collective-permute-start(f32[2,1,8,128]{3,2,1,0:T(8,128)} %get-tuple-element.50), channel_id=1, source_target_pairs={{0,16},{16,0},{1,17},{17,1},{2,18},{18,2},{3,19},{19,3},{4,20},{20... | collective-permute-start | bytes 24584 | tf_op jit(solution)/shard_map/ppermute | solution.py:38
  41.8 22.4 %collective-permute-start.3 = (f32[18,18,128]{2,1,0:T(8,128)}, f32[18,18,128]{2,1,0:T(8,128)}, u32[]{:S(2)}, u32[]{:S(2)}) collective-permute-start(f32[18,18,128]{2,1,0:T(8,128)} %bitcast.34), channel_id=1, source_target_pairs={{4,0},{8,4},{12,8},{5,1},{9,5},{13,9},{6,2},{10,6},{14,10},{7,3},{... | collective-permute-start | bytes 497672 | tf_op jit(solution)/shard_map/ppermute | solution.py:29
  43.2 6.8 %collective-permute-start.7 = (f32[2,6,1,128]{3,2,1,0:T(1,128)S(1)}, f32[2,6,1,128]{3,2,1,0:T(1,128)S(1)}, u32[]{:S(2)}, u32[]{:S(2)}) collective-permute-start(f32[2,6,1,128]{3,2,1,0:T(1,128)S(1)} %get-tuple-element.43), channel_id=1, source_target_pairs={{4,0},{8,4},{12,8},{0,12},{5,1},{9,5},{13,9},{1,13},{6,2},{10,6},{... | collective-permute-start | bytes 18440 | tf_op jit(solution)/shard_map/ppermute | solution.py:41
  48.5 5.4 %collective-permute-start.6 = (f32[2,6,1,128]{3,2,1,0:T(1,128)S(1)}, f32[2,6,1,128]{3,2,1,0:T(1,128)S(1)}, u32[]{:S(2)}, u32[]{:S(2)}) collective-permute-start(f32[2,6,1,128]{3,2,1,0:T(1,128)S(1)} %get-tuple-element.42), channel_id=1, source_target_pairs={{0,4},{4,8},{8,12},{12,0},{1,5},{5,9},{9,13},{13,1},{2,6},{6,10},{... | collective-permute-start | bytes 18440 | tf_op jit(solution)/shard_map/ppermute | solution.py:38
  54.7 6.9 %collective-permute-start.9 = (f32[2,6,10,1]{3,2,1,0:T(8,128)}, f32[2,6,10,1]{3,2,1,0:T(8,128)}, u32[]{:S(2)}, u32[]{:S(2)}) collective-permute-start(f32[2,6,10,1]{3,2,1,0:T(8,128)} %get-tuple-element.33), channel_id=1, source_target_pairs={{1,0},{2,1},{3,2},{0,3},{5,4},{6,5},{7,6},{4,7},{9,8},{10,9},{11,1... | collective-permute-start | bytes 1448 | tf_op jit(solution)/shard_map/ppermute | solution.py:41
  54.7 6.9 %collective-permute-start.8 = (f32[2,6,10,1]{3,2,1,0:T(8,128)}, f32[2,6,10,1]{3,2,1,0:T(8,128)}, u32[]{:S(2)}, u32[]{:S(2)}) collective-permute-start(f32[2,6,10,1]{3,2,1,0:T(8,128)} %get-tuple-element.32), channel_id=1, source_target_pairs={{0,1},{1,2},{2,3},{3,0},{4,5},{5,6},{6,7},{7,4},{8,9},{9,10},{10,1... | collective-permute-start | bytes 1448 | tf_op jit(solution)/shard_map/ppermute | solution.py:38
  83.8 3.7 %collective-permute-start.11 = (f32[2,1,8,128]{3,2,1,0:T(8,128)S(1)}, f32[2,1,8,128]{3,2,1,0:T(8,128)S(1)}, u32[]{:S(2)}, u32[]{:S(2)}) collective-permute-start(f32[2,1,8,128]{3,2,1,0:T(8,128)S(1)} %get-tuple-element.49), channel_id=1, source_target_pairs={{16,0},{0,16},{17,1},{1,17},{18,2},{2,18},{19,3},{3,19},{20,4},{4,... | collective-permute-start | bytes 24584 | tf_op jit(solution)/shard_map/ppermute | solution.py:41
  84.3 3.7 %collective-permute-start.10 = (f32[2,1,8,128]{3,2,1,0:T(8,128)S(1)}, f32[2,1,8,128]{3,2,1,0:T(8,128)S(1)}, u32[]{:S(2)}, u32[]{:S(2)}) collective-permute-start(f32[2,1,8,128]{3,2,1,0:T(8,128)S(1)} %get-tuple-element.48), channel_id=1, source_target_pairs={{0,16},{16,0},{1,17},{17,1},{2,18},{18,2},{3,19},{19,3},{4,20},{20... | collective-permute-start | bytes 24584 | tf_op jit(solution)/shard_map/ppermute | solution.py:38
  88.0 3.7 %collective-permute-start.13 = (f32[2,6,1,128]{3,2,1,0:T(1,128)S(1)}, f32[2,6,1,128]{3,2,1,0:T(1,128)S(1)}, u32[]{:S(2)}, u32[]{:S(2)}) collective-permute-start(f32[2,6,1,128]{3,2,1,0:T(1,128)S(1)} %get-tuple-element.41), channel_id=1, source_target_pairs={{4,0},{8,4},{12,8},{0,12},{5,1},{9,5},{13,9},{1,13},{6,2},{10,6},{... | collective-permute-start | bytes 18440 | tf_op jit(solution)/shard_map/ppermute | solution.py:41
  88.1 5.5 %collective-permute-start.12 = (f32[2,6,1,128]{3,2,1,0:T(1,128)S(1)}, f32[2,6,1,128]{3,2,1,0:T(1,128)S(1)}, u32[]{:S(2)}, u32[]{:S(2)}) collective-permute-start(f32[2,6,1,128]{3,2,1,0:T(1,128)S(1)} %get-tuple-element.40), channel_id=1, source_target_pairs={{0,4},{4,8},{8,12},{12,0},{1,5},{5,9},{9,13},{13,1},{2,6},{6,10},{... | collective-permute-start | bytes 18440 | tf_op jit(solution)/shard_map/ppermute | solution.py:38
  93.7 5.1 %collective-permute-start.14 = (f32[2,6,10,1]{3,2,1,0:T(8,128)S(1)}, f32[2,6,10,1]{3,2,1,0:T(8,128)S(1)}, u32[]{:S(2)}, u32[]{:S(2)}) collective-permute-start(f32[2,6,10,1]{3,2,1,0:T(8,128)S(1)} %get-tuple-element.30), channel_id=1, source_target_pairs={{0,1},{1,2},{2,3},{3,0},{4,5},{5,6},{6,7},{7,4},{8,9},{9,10},{10,1... | collective-permute-start | bytes 1448 | tf_op jit(solution)/shard_map/ppermute | solution.py:38
  99.4 3.7 %collective-permute-start.17 = (f32[2,1,8,128]{3,2,1,0:T(8,128)S(1)}, f32[2,1,8,128]{3,2,1,0:T(8,128)S(1)}, u32[]{:S(2)}, u32[]{:S(2)}) collective-permute-start(f32[2,1,8,128]{3,2,1,0:T(8,128)S(1)} %get-tuple-element.47), channel_id=1, source_target_pairs={{16,0},{0,16},{17,1},{1,17},{18,2},{2,18},{19,3},{3,19},{20,4},{4,... | collective-permute-start | bytes 24584 | tf_op jit(solution)/shard_map/ppermute | solution.py:41
  101.0 3.7 %collective-permute-start.16 = (f32[2,1,8,128]{3,2,1,0:T(8,128)S(1)}, f32[2,1,8,128]{3,2,1,0:T(8,128)S(1)}, u32[]{:S(2)}, u32[]{:S(2)}) collective-permute-start(f32[2,1,8,128]{3,2,1,0:T(8,128)S(1)} %get-tuple-element.46), channel_id=1, source_target_pairs={{0,16},{16,0},{1,17},{17,1},{2,18},{18,2},{3,19},{19,3},{4,20},{20... | collective-permute-start | bytes 24584 | tf_op jit(solution)/shard_map/ppermute | solution.py:38
  104.6 3.7 %collective-permute-start.19 = (f32[2,6,1,128]{3,2,1,0:T(1,128)S(1)}, f32[2,6,1,128]{3,2,1,0:T(1,128)S(1)}, u32[]{:S(2)}, u32[]{:S(2)}) collective-permute-start(f32[2,6,1,128]{3,2,1,0:T(1,128)S(1)} %get-tuple-element.39), channel_id=1, source_target_pairs={{4,0},{8,4},{12,8},{0,12},{5,1},{9,5},{13,9},{1,13},{6,2},{10,6},{... | collective-permute-start | bytes 18440 | tf_op jit(solution)/shard_map/ppermute | solution.py:41
  104.7 5.5 %collective-permute-start.18 = (f32[2,6,1,128]{3,2,1,0:T(1,128)S(1)}, f32[2,6,1,128]{3,2,1,0:T(1,128)S(1)}, u32[]{:S(2)}, u32[]{:S(2)}) collective-permute-start(f32[2,6,1,128]{3,2,1,0:T(1,128)S(1)} %get-tuple-element.38), channel_id=1, source_target_pairs={{0,4},{4,8},{8,12},{12,0},{1,5},{5,9},{9,13},{13,1},{2,6},{6,10},{... | collective-permute-start | bytes 18440 | tf_op jit(solution)/shard_map/ppermute | solution.py:38
  110.3 4.1 %collective-permute-start.20 = (f32[2,6,10,1]{3,2,1,0:T(8,128)S(1)}, f32[2,6,10,1]{3,2,1,0:T(8,128)S(1)}, u32[]{:S(2)}, u32[]{:S(2)}) collective-permute-start(f32[2,6,10,1]{3,2,1,0:T(8,128)S(1)} %get-tuple-element.28), channel_id=1, source_target_pairs={{0,1},{1,2},{2,3},{3,0},{4,5},{5,6},{6,7},{7,4},{8,9},{9,10},{10,1... | collective-permute-start | bytes 1448 | tf_op jit(solution)/shard_map/ppermute | solution.py:38
  115.0 3.7 %collective-permute-start.23 = (f32[2,1,8,128]{3,2,1,0:T(8,128)S(1)}, f32[2,1,8,128]{3,2,1,0:T(8,128)S(1)}, u32[]{:S(2)}, u32[]{:S(2)}) collective-permute-start(f32[2,1,8,128]{3,2,1,0:T(8,128)S(1)} %get-tuple-element.45), channel_id=1, source_target_pairs={{16,0},{0,16},{17,1},{1,17},{18,2},{2,18},{19,3},{3,19},{20,4},{4,... | collective-permute-start | bytes 24584 | tf_op jit(solution)/shard_map/ppermute | solution.py:41
  119.2 3.7 %collective-permute-start.25 = (f32[2,6,1,128]{3,2,1,0:T(1,128)S(1)}, f32[2,6,1,128]{3,2,1,0:T(1,128)S(1)}, u32[]{:S(2)}, u32[]{:S(2)}) collective-permute-start(f32[2,6,1,128]{3,2,1,0:T(1,128)S(1)} %get-tuple-element.37), channel_id=1, source_target_pairs={{4,0},{8,4},{12,8},{0,12},{5,1},{9,5},{13,9},{1,13},{6,2},{10,6},{... | collective-permute-start | bytes 18440 | tf_op jit(solution)/shard_map/ppermute | solution.py:41
  119.3 5.5 %collective-permute-start.24 = (f32[2,6,1,128]{3,2,1,0:T(1,128)S(1)}, f32[2,6,1,128]{3,2,1,0:T(1,128)S(1)}, u32[]{:S(2)}, u32[]{:S(2)}) collective-permute-start(f32[2,6,1,128]{3,2,1,0:T(1,128)S(1)} %get-tuple-element.36), channel_id=1, source_target_pairs={{0,4},{4,8},{8,12},{12,0},{1,5},{5,9},{9,13},{13,1},{2,6},{6,10},{... | collective-permute-start | bytes 18440 | tf_op jit(solution)/shard_map/ppermute | solution.py:38
  125.0 5.1 %collective-permute-start.26 = (f32[2,6,10,1]{3,2,1,0:T(8,128)S(1)}, f32[2,6,10,1]{3,2,1,0:T(8,128)S(1)}, u32[]{:S(2)}, u32[]{:S(2)}) collective-permute-start(f32[2,6,10,1]{3,2,1,0:T(8,128)S(1)} %get-tuple-element.26), channel_id=1, source_target_pairs={{0,1},{1,2},{2,3},{3,0},{4,5},{5,6},{6,7},{7,4},{8,9},{9,10},{10,1... | collective-permute-start | bytes 1448 | tf_op jit(solution)/shard_map/ppermute | solution.py:38
  (35 other events, 376.5 us)
where the time goes:
time: 132 us; the launch traced here: 131 us
  waiting for transfers between devices  36 us (27%)
  local copies, waits for them, and re-layouts  30.6 us (23%)
  starting transfers between devices  30 us (23%)
  other arithmetic  18.3 us (14%)
  blocking collectives  13.1 us (10%)
  matrix products  1.67 us (1%)
  between operations  1.33 us (1%)
    ppermute x12, waiting for transfers between devices, padded(): lax.ppermute(lax.slice_in_dim(block, block.shape[dim] - width, None, axis...  19 us
    ppermute x12, waiting for transfers between devices, padded(): lax.ppermute(lax.slice_in_dim(block, 0, width, axis=dim), axis, backward)  17 us
    ppermute x12, starting transfers between devices, padded(): lax.ppermute(lax.slice_in_dim(block, block.shape[dim] - width, None, axis...  12.1 us
    ppermute x12, starting transfers between devices, padded(): lax.ppermute(lax.slice_in_dim(block, 0, width, axis=dim), axis, backward)  10 us
    psum x1, blocking collectives, shards(): coupling = lax.psum(partial_value, 'sec').reshape(4, tile_rows, tile_cols)  8.16 us
    unnamed x67, local copies, waits for them, and re-layouts  8.11 us
    mul x1, other arithmetic, wave_update(): return sea_cells * (advected * doppler)  6.62 us
    ppermute x2, starting transfers between devices, passed_along_2(): lax.ppermute(value, axis, [(source, source + steps) for source in range(l...  5.56 us
  transfers between devices with their start and end apart: 28, of which 20 were waited for; matrix products, arithmetic and copies ran while one was open for 23% of the time, Pallas kernels for 0%

commit v1 on v0

v1 whole, which is shorter than its diff:
```python
import functools
import math

import jax
import jax.numpy as jnp
import numpy as np
from jax import lax
from jax.experimental import pallas as pl
from jax.experimental.pallas import tpu as pltpu
from jax.sharding import PartitionSpec as P

ITERS = 4
ROWS = 8
LANES = 128
HALO = 4
MOMENTS = 5
SUMS = 2 * MOMENTS
FLUX_COLS = 3
current_gain = 0.1
stress_gain = 0.5

VMEM = pl.BlockSpec(memory_space=pltpu.VMEM)
SMEM = pl.BlockSpec(memory_space=pltpu.SMEM)
ANY = pl.BlockSpec(memory_space=pl.ANY)
F32 = jnp.float32


def lanes():
    return lax.broadcasted_iota(jnp.int32, (ROWS, LANES), 1)


def rows():
    return lax.broadcasted_iota(jnp.int32, (ROWS, LANES), 0)


def lane_roll(tile, shift):
    if isinstance(shift, int):
        shift %= LANES
        if shift == 0:
            return tile
    return pltpu.roll(tile, shift, 1)


def row_roll(tile, shift):
    shift %= ROWS
    return tile if shift == 0 else pltpu.roll(tile, shift, 0)


def spread(ref, row):
    return jnp.broadcast_to(ref[pl.ds(row, 1), :], (ROWS, LANES))


def put(ref, index, tile):
    ref[pl.ds(index * ROWS, ROWS), :] = tile


def take(ref, index):
    return ref[pl.ds(index * ROWS, ROWS), :]


def coupled(sums, zonal, meridional, sea):
    result = []
    for w in range(2):
        c, s, cc, cs, ss = sums[w * MOMENTS : (w + 1) * MOMENTS]
        result.append(sea * (c + current_gain * (zonal * cc + meridional * cs)))
        result.append(sea * (s + current_gain * (zonal * cs + meridional * ss)))
    return result


class Sizes:
    def __init__(self, freqs, directions, levels):
        self.freqs = freqs
        self.directions = directions
        self.levels = levels
        self.quarter = directions // 4
        self.fields = 2 * 2 * levels
        self.half = directions // 2
        self.per_tile = LANES // self.half
        self.col_tiles = -(-freqs // self.per_tile)
        self.edge_rows = freqs * directions // 2
        self.sec_sums = self.fields // 2
        self.sec_cols = self.sec_sums + SUMS
        self.sec_rows = self.sec_cols + 1
        self.sec_tiles = self.sec_rows + -(-2 * SUMS // ROWS)
        self.lon_coup = HALO * (self.fields + 2)
        self.lon_flux = self.lon_coup + 4 * HALO
        self.lon_rows = self.lon_flux + SUMS
        self.arrays = self.fields + 2 + 4
        self.pairs = self.arrays // 2
        self.flux_tiles = -(-SUMS // ROWS)
        self.lat_pairs = 0
        self.lat_flux = self.lat_pairs + self.pairs
        self.lat_edges = self.lat_flux + self.flux_tiles
        self.lat_tiles = self.lat_edges + 1
        self.coef_tiles = -(-freqs // ROWS)
        assert self.lon_rows + SUMS * FLUX_COLS <= LANES
        assert (self.pairs + self.flux_tiles) * 2 * HALO <= LANES

    def headings(self, i):
        q = self.quarter
        return (i, 2 * q - 1 - i, 2 * q + i, 4 * q - 1 - i)


def chunks(z):
    q = z.quarter
    group = 3 if q % 3 == 0 else 1
    result = []
    for lo in range(0, q, group):
        hi = lo + group
        result.append((lo, hi, [pl.ds(start, group) for start in (lo, 2 * q - hi, 2 * q + lo, 4 * q - hi)]))
    return result


def sums_kernel(z, x, cur_in, mask_in, diffusion_in, courant_in, stokes_in, stress_in, table_in, buf, pay, first_rows, second_rows, ecol, wcol, local, coef, cur, mask, courant, stokes, stress, table, acc, sems, small_sems):
    q, nf = z.quarter, z.freqs
    pairs = ((cur_in, cur), (mask_in, mask), (diffusion_in, local.at[pl.ds(ROWS, ROWS)]), (courant_in, courant), (stokes_in, stokes), (stress_in, stress), (table_in, table))
    small = [pltpu.make_async_copy(source, target, small_sems.at[k]) for k, (source, target) in enumerate(pairs)]
    for copy in small:
        copy.start()
    copies = []
    for g, (_, _, spans) in enumerate(chunks(z)):
        for j, span in enumerate(spans):
            copies.append(pltpu.make_async_copy(x.at[:, span], buf.at[:, span], sems.at[4 * g + j]))
    for copy in copies:
        copy.start()

    lane, row = lanes(), rows()
    zero = jnp.zeros((ROWS, LANES), F32)
    for k in range(5 * SUMS):
        acc[k] = zero
    for t in range(z.col_tiles):
        put(ecol, t, zero)
        put(wcol, t, zero)
    for copy in small:
        copy.wait()
    sea = mask[...].astype(F32)
    put(local, 0, sea)
    for comp in range(2):
        for level in range(z.levels):
            put(pay, comp * z.levels + level, cur[comp, level] * sea)
    for f in range(nf):
        coef[pl.ds(f, 1), :] = jnp.full((1, LANES), courant[f], F32)

    def body(i, _):
        c, s = table[0, i], table[1, i]
        heading = z.headings(i)
        total = [[zero] * 4 for _ in range(4)]
        east, west = [zero] * z.col_tiles, [zero] * z.col_tiles
        for f in range(nf):
            t = f // z.per_tile
            cg = courant[f]
            factors = (stokes[f], stokes[f] * cg, stress[f], stress[f] * cg)
            for j in range(4):
                energy = buf[f, heading[j]]
                for k in range(4):
                    total[k][j] = total[k][j] + factors[k] * energy
                at = f % z.per_tile * z.half + (0 if j in (0, 1) else 1)
                if j in (0, 3):
                    east[t] = jnp.where(lane == at, lane_roll(energy, at - (LANES - 1)), east[t])
                else:
                    west[t] = jnp.where(lane == at, lane_roll(energy, at), west[t])
        mine = lax.div(lax.rem(lane, z.half), 2) == i
        for ref, tiles in ((ecol, east), (wcol, west)):
            for t in range(z.col_tiles):
                put(ref, t, jnp.where(mine, lane_roll(tiles[t], 2 * i), take(ref, t)))
        cc, cs, ss = c * c, c * s, s * s
        for w in range(2):
            plain, fast = total[2 * w], total[2 * w + 1]
            both = c + s
            h = [plain[j] - both * fast[j] for j in range(4)]
            here, there = h[0] + h[3], h[1] + h[2]
            every = here + there
            values = [
                c * (here - there),
                s * ((h[0] + h[1]) - (h[2] + h[3])),
                cc * every,
                cs * ((h[0] - h[3]) + (h[2] - h[1])),
                ss * every,
            ]
            for a, b, size, signs in (
                (fast[0] + fast[3], fast[0] - fast[3], c, (1, 1, 1)),
                (fast[1] + fast[2], fast[1] - fast[2], c, (-1, 1, -1)),
            ):
                values += [signs[0] * size * c * a, signs[1] * size * s * b, size * cc * a, signs[2] * size * cs * b, size * ss * a]
            for a, b, size, signs in (
                (fast[0] + fast[1], fast[0] - fast[1], s, (1, 1, 1)),
                (fast[2] + fast[3], fast[3] - fast[2], s, (1, -1, -1)),
            ):
                values += [signs[0] * size * c * b, signs[1] * size * s * a, size * cc * a, signs[2] * size * cs * b, size * ss * a]
            for kind in range(5):
                for m in range(MOMENTS):
                    at = kind * SUMS + w * MOMENTS + m
                    acc[at] = acc[at] + values[kind * MOMENTS + m]
        return 0

    for g, (lo, hi, _) in enumerate(chunks(z)):
        for copy in copies[4 * g : 4 * g + 4]:
            copy.wait()
        lax.fori_loop(lo, hi, body, 0)

    flat = buf.reshape(nf * z.directions * ROWS, LANES)
    odd = lax.rem(lax.axis_index("lat"), 2)
    north, south = ROWS - 1, z.half * ROWS
    for ref, start in ((first_rows, north + odd * (south - north)), (second_rows, south + odd * (north - south))):
        for f in range(nf):
            ref[pl.ds(f * z.half, z.half), :] = flat[pl.ds(f * z.directions * ROWS + start, z.half, stride=ROWS), :]

    cols = zero
    for k in range(SUMS):
        center, east, west, north, south = (acc[kind * SUMS + k] for kind in range(5))
        value = center + jnp.where(lane > 0, lane_roll(east, 1), 0.0) + jnp.where(lane < LANES - 1, lane_roll(west, -1), 0.0)
        value = value + jnp.where(row > 0, row_roll(north, 1), 0.0) + jnp.where(row < ROWS - 1, row_roll(south, -1), 0.0)
        put(pay, z.sec_sums + k, value)
        cols = jnp.where(lane == k, lane_roll(east, k - (LANES - 1)), cols)
        cols = jnp.where(lane == SUMS + k, lane_roll(west, SUMS + k), cols)
        pay[pl.ds(z.sec_rows * ROWS + k, 1), :] = north[ROWS - 1 :]
        pay[pl.ds(z.sec_rows * ROWS + SUMS + k, 1), :] = south[:1]
    put(pay, z.sec_cols, cols)
    spare = (z.sec_tiles - z.sec_rows) * ROWS - 2 * SUMS
    if spare:
        pay[pl.ds(z.sec_tiles * ROWS - spare, spare), :] = jnp.zeros((spare, LANES), F32)


def columns_kernel(z, mine, other, local, ecol, wcol, second_rows, fields, coup, flux, to_east, to_west, second_out):
    lane, row = lanes(), rows()
    sec = lax.axis_index("sec")
    total = 2 * z.levels
    for comp in range(2):
        for level in range(z.levels):
            own = level + sec * (z.levels - 1 - 2 * level)
            far = z.levels + level + sec * (z.levels - 1 - 2 * level)
            fields[comp * total + own] = take(mine, comp * z.levels + level)
            fields[comp * total + far] = take(other, comp * z.levels + level)
    sea, diffusion = take(local, 0), take(local, 1)
    top = sec * (total - 1)
    zonal, meridional = fields[top], fields[total + top]
    sums = [take(mine, z.sec_sums + k) + take(other, z.sec_sums + k) for k in range(SUMS)]
    coupling = coupled(sums, zonal, meridional, sea)
    cols = take(mine, z.sec_cols) + take(other, z.sec_cols)
    put(flux, 0, cols)
    for t in range(z.sec_tiles - z.sec_rows):
        put(flux, 1 + t, take(mine, z.sec_rows + t) + take(other, z.sec_rows + t))
    for k in range(4):
        coup[k] = coupling[k]
    arrays = [fields[k] for k in range(z.fields)] + [sea, diffusion] + coupling
    east, west = lane_roll(cols, z.lon_flux), lane_roll(cols, z.lon_flux - SUMS)
    for k, array in enumerate(arrays):
        mine_here = (lane >= HALO * k) & (lane < HALO * (k + 1))
        east = jnp.where(mine_here, lane_roll(array, HALO * (k + 1)), east)
        west = jnp.where(mine_here, lane_roll(array, HALO * k), west)
    for k in range(SUMS):
        edge = jnp.where(row == ROWS - 1, spread(flux, ROWS + k), spread(flux, ROWS + SUMS + k))
        at = z.lon_rows + FLUX_COLS * k
        mine_here = (lane >= at) & (lane < at + FLUX_COLS)
        east = jnp.where(mine_here, lane_roll(edge, at + FLUX_COLS), east)
        west = jnp.where(mine_here, lane_roll(edge, at), west)
    put(to_east, 0, east)
    put(to_west, 0, west)
    for t in range(z.col_tiles):
        put(to_east, 1 + t, take(ecol, t))
        put(to_west, 1 + t, take(wcol, t))
    second_out[...] = second_rows[...]


def rows_kernel(z, from_west, from_east, fields, coup, flux, local, coup_out, edges, to_first, to_second):
    lane, row = lanes(), rows()
    total = 2 * z.levels
    top = lax.axis_index("sec") * (total - 1)
    sea, diffusion = take(local, 0), take(local, 1)
    cols = take(flux, 0)
    west, east = take(from_west, 0), take(from_east, 0)

    def beyond(first, width):
        near = lane_roll(east, -first)
        far = lane_roll(west, LANES - width - first)
        return jnp.where(lane < width, near, jnp.where(lane >= LANES - width, far, 0.0))

    edge = [beyond(HALO * k, HALO) for k in range(z.fields + 2)]
    for k in range(z.fields + 2):
        edges[k] = edge[k]
    inner, outer = [], []
    for k in range(SUMS):
        at = z.lon_flux + k
        inner.append(jnp.where(lane == 0, lane_roll(west, -at), jnp.where(lane == LANES - 1, lane_roll(east, LANES - 1 - at), 0.0)))
        outer.append(jnp.where(lane == 0, lane_roll(cols, -k), jnp.where(lane == LANES - 1, lane_roll(cols, LANES - 1 - SUMS - k), 0.0)))
    inside = coupled(inner, fields[top], fields[total + top], sea)
    outside = coupled(outer, edges[top], edges[total + top], edge[z.fields])
    main_coupling = [coup[k] + inside[k] for k in range(4)]
    edge_coupling = [beyond(z.lon_coup + HALO * k, HALO) + outside[k] for k in range(4)]
    for k in range(4):
        coup_out[k] = main_coupling[k]
        edges[z.fields + 2 + k] = edge_coupling[k]
    row_edge = [beyond(z.lon_rows + FLUX_COLS * k, FLUX_COLS) for k in range(SUMS)]
    for k in range(SUMS):
        edges[z.arrays + k] = row_edge[k]

    main = [fields[k] for k in range(z.fields)] + [sea, diffusion] + main_coupling
    edge = edge + edge_coupling
    low = row < HALO
    odd = lax.rem(lax.axis_index("lat"), 2) == 1

    def send(index, north, south):
        put(to_first, index, jnp.where(odd, south, north))
        put(to_second, index, jnp.where(odd, north, south))

    def pair(a, b):
        return jnp.where(low, row_roll(b, HALO), a), jnp.where(low, a, row_roll(b, HALO))

    def group(tile, k):
        at = 2 * HALO * k
        in_group = lax.rem(lane + LANES + HALO - at, LANES) < 2 * HALO
        return in_group, lane_roll(tile, at)

    north_edges = jnp.zeros((ROWS, LANES), F32)
    south_edges = north_edges
    for k in range(z.pairs):
        north, south = pair(main[2 * k], main[2 * k + 1])
        send(z.lat_pairs + k, north, south)
        north, south = pair(edge[2 * k], edge[2 * k + 1])
        in_group, moved = group(north, k)
        north_edges = jnp.where(in_group, moved, north_edges)
        in_group, moved = group(south, k)
        south_edges = jnp.where(in_group, moved, south_edges)
    for t in range(z.flux_tiles):
        north, south = jnp.zeros((ROWS, LANES), F32), jnp.zeros((ROWS, LANES), F32)
        north_row, south_row = north, south
        for r in range(min(ROWS, SUMS - t * ROWS)):
            k = t * ROWS + r
            north = jnp.where(row == r, spread(flux, ROWS + k), north)
            south = jnp.where(row == r, spread(flux, ROWS + SUMS + k), south)
            north_row = jnp.where(row == r, jnp.broadcast_to(row_edge[k][ROWS - 1 :], (ROWS, LANES)), north_row)
            south_row = jnp.where(row == r, jnp.broadcast_to(row_edge[k][:1], (ROWS, LANES)), south_row)
        send(z.lat_flux + t, north, south)
        in_group, moved = group(north_row, z.pairs + t)
        north_edges = jnp.where(in_group, moved, north_edges)
        in_group, moved = group(south_row, z.pairs + t)
        south_edges = jnp.where(in_group, moved, south_edges)
    send(z.lat_edges, north_edges, south_edges)


def side_signs(j):
    return (1 if j in (0, 3) else -1), (1 if j in (0, 1) else -1)


def lat_sides(first, second, lat_count):
    place = lax.axis_index("lat")
    odd = lax.rem(place, 2) == 1
    north = jnp.where(place < lat_count - 1, jnp.where(odd, second, first), 0.0)
    south = jnp.where(place > 0, jnp.where(odd, first, second), 0.0)
    return north, south


def wave_kernel(z, lat_count, x, fields, coup, local, coef, from_west, from_east, first, second, out, coup_out, buf, scales, sides, sems):
    q, nf, half = z.quarter, z.freqs, z.half
    lane, row = lanes(), rows()
    total = 2 * z.levels
    top = lax.axis_index("sec") * (total - 1)
    sea = take(local, 0)
    zonal, meridional = current_gain * fields[top], current_gain * fields[total + top]
    coup_out[...] = coup[...]
    sides[0], sides[1] = lat_sides(first[...], second[...], lat_count)
    sizes = tables(z.directions)
    headings = []
    for i in range(q):
        c, s = float(sizes[0, i]), float(sizes[1, i])
        for j, heading in enumerate(z.headings(i)):
            sign_x, sign_y = side_signs(j)
            headings.append((heading, c, s, sign_x, sign_y, 2 * i + (0 if j in (0, 1) else 1)))
            scales[heading] = sea * (1.0 + (sign_x * c) * zonal + (sign_y * s) * meridional)

    def body(f, _):
        speed = spread(coef, f)
        at = pl.ds(pl.multiple_of((1 + lax.div(f, z.per_tile)) * ROWS, ROWS), ROWS)
        back = LANES - half * lax.rem(f, z.per_tile)
        west, east = lane_roll(from_west[at, :], back), lane_roll(from_east[at, :], back)
        for heading, c, s, sign_x, sign_y, k in headings:
            energy = x[f, heading]
            if sign_x > 0:
                beside = jnp.where(lane == 0, lane_roll(west, -k), lane_roll(energy, 1))
            else:
                beside = jnp.where(lane == LANES - 1, lane_roll(east, LANES - 1 - k), lane_roll(energy, -1))
            if sign_y > 0:
                below = jnp.where(row == 0, spread(sides.at[1], f * half + heading), row_roll(energy, 1))
            else:
                below = jnp.where(row == ROWS - 1, spread(sides.at[0], f * half + heading - half), row_roll(energy, -1))
            step = c * (beside - energy) + s * (below - energy)
            buf[f, heading] = scales[heading] * (energy + speed * step)
        return 0

    parts = 3 if nf % 3 == 0 else 1
    copies = []
    for g in range(parts):
        span = pl.ds(g * (nf // parts), nf // parts)
        lax.fori_loop(g * (nf // parts), (g + 1) * (nf // parts), body, 0)
        copy = pltpu.make_async_copy(buf.at[span], out.at[span], sems.at[g])
        copy.start()
        copies.append(copy)
    for copy in copies:
        copy.wait()


def ocean_kernel(z, lat_count, from_first, from_second, fields, coup, flux, edges, local, currents_out, ext, force):
    total = 2 * z.levels
    row = rows()
    sec = lax.axis_index("sec")
    top = sec * (total - 1)
    sea, diffusion = take(local, 0), take(local, 1)
    low = row < HALO

    def pair(north, south):
        first = jnp.where(low, north, south)
        second = jnp.where(low, row_roll(north, HALO), row_roll(south, HALO))
        return first, second

    def sides(index):
        return lat_sides(take(from_first, index), take(from_second, index), lat_count)

    north_edges, south_edges = sides(z.lat_edges)
    north_rows, south_rows = zip(*[sides(z.lat_flux + t) for t in range(z.flux_tiles)])
    halo, halo_edge = [], []
    for k in range(z.pairs):
        halo += pair(*sides(z.lat_pairs + k))
        halo_edge += pair(lane_roll(north_edges, -2 * HALO * k), lane_roll(south_edges, -2 * HALO * k))
    inner, outer, inner_edge, outer_edge = [], [], [], []
    for k in range(SUMS):
        t, r = k // ROWS, k % ROWS
        high = row == ROWS - 1
        bottom = row == 0
        north = jnp.broadcast_to(north_rows[t][r : r + 1], (ROWS, LANES))
        south = jnp.broadcast_to(south_rows[t][r : r + 1], (ROWS, LANES))
        inner.append(jnp.where(high, north, jnp.where(bottom, south, 0.0)))
        outer.append(jnp.where(bottom, spread(flux, ROWS + k), jnp.where(high, spread(flux, ROWS + SUMS + k), 0.0)))
        shift = -2 * HALO * (z.pairs + t)
        north = jnp.broadcast_to(lane_roll(north_edges, shift)[r : r + 1], (ROWS, LANES))
        south = jnp.broadcast_to(lane_roll(south_edges, shift)[r : r + 1], (ROWS, LANES))
        inner_edge.append(jnp.where(high, north, jnp.where(bottom, south, 0.0)))
        mine = edges[z.arrays + k]
        outer_edge.append(
            jnp.where(bottom, jnp.broadcast_to(mine[ROWS - 1 :], (ROWS, LANES)), jnp.where(high, jnp.broadcast_to(mine[:1], (ROWS, LANES)), 0.0))
        )

    def joined(main, edge, halo_main, halo_side):
        return jnp.concatenate([jnp.concatenate([main, edge], axis=1), jnp.concatenate([halo_main, halo_side], axis=1)], axis=0)

    for k in range(z.fields):
        ext[k] = joined(fields[k], edges[k], halo[k], halo_edge[k])
    sea_all = joined(sea, edges[z.fields], halo[z.fields], halo_edge[z.fields])
    kappa = joined(diffusion, edges[z.fields + 1], halo[z.fields + 1], halo_edge[z.fields + 1])
    sums = [joined(inner[k], inner_edge[k], outer[k], outer_edge[k]) for k in range(SUMS)]
    extra = coupled(sums, ext[top], ext[total + top], sea_all)
    first = z.fields + 2
    coupling = [joined(coup[k], edges[first + k], halo[first + k], halo_edge[first + k]) + extra[k] for k in range(4)]

    shape = (2 * ROWS, 2 * LANES)
    row_all = lax.broadcasted_iota(jnp.int32, shape, 0)
    row_all = jnp.where(row_all >= 2 * ROWS - HALO, row_all - 2 * ROWS, row_all) + lax.axis_index("lat") * ROWS
    rot = sea_all * (0.05 + 0.1 * (row_all.astype(F32) + 0.5) / (lat_count * ROWS))
    spin = sea_all * kappa

    def level_of(p):
        return p + sec * (total - 1 - 2 * p)

    mixes, centers = [], []
    for p in range(total):
        level = level_of(p)
        mixes.append(0.04 + 0.0125 * lax.rem(7 * level, 5).astype(F32))
        decay = 1.0 / (1.0 + jnp.full(shape, level, jnp.int32).astype(F32))
        gain = jnp.where(level == 0, stress_gain, 0.0)
        force[p] = rot * decay * coupling[1] + sea_all * gain * coupling[2]
        force[total + p] = sea_all * gain * coupling[3] - rot * decay * coupling[0]
    for step in range(ITERS):
        needed = min(total, z.levels + ITERS - 1 - step)
        after = []
        for comp in range(2):
            for p in range(needed):
                value = ext[comp * total + p]
                ring = (pltpu.roll(value, 1, 1) + pltpu.roll(value, 2 * LANES - 1, 1)) + (pltpu.roll(value, 1, 0) + pltpu.roll(value, 2 * ROWS - 1, 0))
                near = [ext[comp * total + other] for other in (p - 1, p + 1) if 0 <= other < total]
                column = near[0] - value if len(near) == 1 else near[0] + near[1] - 2.0 * value
                turned = ext[(1 - comp) * total + p]
                turned = rot * turned if comp == 0 else -(rot * turned)
                after.append(sea_all * (value + mixes[p] * column) + spin * (ring - 4.0 * value) + turned + force[comp * total + p])
        if step < ITERS - 1:
            for comp in range(2):
                for p in range(needed):
                    ext[comp * total + p] = after[comp * needed + p]
        else:
            for comp in range(2):
                for level in range(z.levels):
                    own = level
                    place = level + sec * (z.levels - 1 - 2 * level)
                    currents_out[comp, place] = after[comp * needed + own][:ROWS, :LANES]


def tables(directions):
    quarter = directions // 4
    heading = (np.arange(quarter) + 0.5) * (2.0 * math.pi / directions)
    return np.stack([np.cos(heading), np.sin(heading)]).astype(np.float32)


def shifted(value, axis, steps):
    count = lax.axis_size(axis)
    return lax.ppermute(value, axis, [(i, (i + steps) % count) for i in range(count)])


def swapped(value, parity):
    lat, lon = lax.axis_size("lat"), lax.axis_size("lon")
    pairs = []
    for i in range(lat):
        other = i + 1 if i % 2 == parity else i - 1
        for j in range(lon):
            if 0 <= other < lat:
                pairs.append((i * lon + j, other * lon + j))
            elif j ^ 1 < lon:
                pairs.append((i * lon + j, i * lon + (j ^ 1)))
    return lax.ppermute(value, ("lat", "lon"), pairs)


def flat(tiles):
    return jax.ShapeDtypeStruct((tiles * ROWS, LANES), F32)


def stack(count):
    return jax.ShapeDtypeStruct((count, ROWS, LANES), F32)


def call(kernel, out_shape, in_specs, out_specs=None, scratch=(), name=None, bytes_accessed=0, flops=0):
    return pl.pallas_call(
        kernel,
        out_shape=out_shape,
        in_specs=in_specs,
        out_specs=out_specs if out_specs is not None else [VMEM] * len(out_shape),
        scratch_shapes=list(scratch),
        name=name,
        compiler_params=pltpu.CompilerParams(vmem_limit_bytes=24 * 1024 * 1024),
        cost_estimate=pl.CostEstimate(flops=flops, bytes_accessed=bytes_accessed, transcendentals=0),
    )


def shards(spectra, currents, land_mask, diffusion, courant, stokes_weight, stress_weight):
    freqs, directions, tile_rows, tile_cols = spectra.shape
    levels = currents.shape[1]
    lat_count = lax.axis_size("lat")
    assert lax.axis_size("sec") == 2 and (tile_rows, tile_cols) == (ROWS, LANES) and directions % 4 == 0
    z = Sizes(freqs, directions, levels)
    table = jnp.asarray(tables(directions))
    size = spectra.size * 4
    copies = 4 * len(chunks(z))
    sems = pltpu.SemaphoreType.DMA((copies,))
    whole = pltpu.VMEM(spectra.shape, F32)

    edge_rows = jax.ShapeDtypeStruct((z.edge_rows, LANES), F32)
    inputs = (spectra, currents, land_mask, diffusion, courant, stokes_weight, stress_weight, table)
    kept, pay, first_rows, second_rows, ecol, wcol, local, coef = call(
        functools.partial(sums_kernel, z),
        (whole, flat(z.sec_tiles), edge_rows, edge_rows, flat(z.col_tiles), flat(z.col_tiles), flat(2), flat(z.coef_tiles)),
        [ANY] * 8,
        scratch=[
            pltpu.VMEM(currents.shape, F32),
            pltpu.VMEM(land_mask.shape, jnp.int32),
            pltpu.SMEM(courant.shape, F32),
            pltpu.SMEM(courant.shape, F32),
            pltpu.SMEM(courant.shape, F32),
            pltpu.SMEM(table.shape, F32),
            pltpu.VMEM((5 * SUMS, ROWS, LANES), F32),
            sems,
            pltpu.SemaphoreType.DMA((7,)),
        ],
        name="spectra_sums",
        bytes_accessed=size,
        flops=16 * size // 4,
    )(*[pltpu.with_memory_space_constraint(array, pltpu.HBM) for array in inputs])

    got_first = swapped(first_rows, 0)
    other = shifted(pay, "sec", 1)

    fields, coup, flux, to_east, to_west, second_rows = call(
        functools.partial(columns_kernel, z),
        (stack(z.fields), stack(4), flat(1 + z.sec_tiles - z.sec_rows), flat(1 + z.col_tiles), flat(1 + z.col_tiles), edge_rows),
        [VMEM] * 6,
        name="pack_columns",
        bytes_accessed=2**18,
        flops=2**16,
    )(pay, other, local, ecol, wcol, second_rows)

    got_second = swapped(second_rows, 1)
    from_east = shifted(to_west, "lon", -1)
    from_west = shifted(to_east, "lon", 1)

    coup, edges, to_first, to_second = call(
        functools.partial(rows_kernel, z),
        (stack(4), stack(z.arrays + SUMS), flat(z.lat_tiles), flat(z.lat_tiles)),
        [VMEM] * 6,
        name="pack_rows",
        bytes_accessed=2**18,
        flops=2**16,
    )(from_west, from_east, fields, coup, flux, local)

    from_second = swapped(to_second, 1)
    from_first = swapped(to_first, 0)

    new_spectra, coup = call(
        functools.partial(wave_kernel, z, lat_count),
        (jax.ShapeDtypeStruct(spectra.shape, F32), stack(4)),
        [VMEM] * 9,
        out_specs=[ANY, VMEM],
        scratch=[whole, pltpu.VMEM((directions, ROWS, LANES), F32), pltpu.VMEM((2, z.edge_rows, LANES), F32), sems],
        name="wave_step",
        bytes_accessed=2 * size,
        flops=9 * size // 4,
    )(kept, fields, coup, local, coef, from_west, from_east, got_first, got_second)

    (new_currents,) = call(
        functools.partial(ocean_kernel, z, lat_count),
        (jax.ShapeDtypeStruct(currents.shape, F32),),
        [VMEM] * 7,
        scratch=[pltpu.VMEM((z.fields, 2 * ROWS, 2 * LANES), F32), pltpu.VMEM((z.fields, 2 * ROWS, 2 * LANES), F32)],
        name="ocean_steps",
        bytes_accessed=2**20,
        flops=2**20,
    )(from_first, from_second, fields, coup, flux, edges, local)
    return new_spectra, new_currents


def solution(mesh):
    in_specs = (
        P("sec", None, "lat", "lon"),
        P(None, "sec", "lat", "lon"),
        P("lat", "lon"),
        P("lat", "lon"),
        P("sec"),
        P("sec"),
        P("sec"),
    )
    out_specs = (P("sec", None, "lat", "lon"), P(None, "sec", "lat", "lon"))
    return jax.shard_map(shards, mesh=mesh, in_specs=in_specs, out_specs=out_specs, check_vma=False)
```

time: 132 us -> 25.2 us (0.19)
  waiting for transfers between devices: 36 us -> 2.5 us
  local copies, waits for them, and re-layouts: 30.6 us -> 0 us
  starting transfers between devices: 30 us -> 11.3 us
  other arithmetic: 18.3 us -> 0 us
  blocking collectives: 13.1 us -> 0 us
  Pallas kernels: 0 us -> 10.5 us
  matrix products: 1.67 us -> 0 us
    ppermute x28 -> x7, waiting for transfers between devices: 36 us -> 2.5 us  [the longest x3 2.48 us: shifted(): lax.ppermute(value, axis, [(i, (i + steps) % count) for i in range(count)])]
    ppermute x28 -> x7, starting transfers between devices: 30 us -> 11.3 us  [the longest x4 6.28 us: swapped(): return lax.ppermute(value, ('lat', 'lon'), pairs)]
    psum x2 -> x0, blocking collectives: 13.1 us -> none  [the longest x1 8.16 us: shards(): coupling = lax.psum(partial_value, 'sec').reshape(4, tile_rows, tile_cols)]
    slice x12 -> x0, local copies, waits for them, and re-layouts: 12 us -> none  [the longest x1 3.25 us: shards(): spectra[:, :, :, 1:]]
    pallas_call x0 -> x5, Pallas kernels: none -> 10.5 us  [the longest x1 5.19 us: shards(): call(functools.partial(wave_kernel, z, lat_count), (jax.ShapeDtypeStruct(...]
    mul x11 -> x0, other arithmetic: 10.2 us -> none  [the longest x1 6.62 us: wave_update(): return sea_cells * (advected * doppler)]
    unnamed x67 -> x0, local copies, waits for them, and re-layouts: 8.11 us -> none
    broadcast_in_dim x8 -> x0, local copies, waits for them, and re-layouts: 7.02 us -> none  [the longest x1 2.72 us: shards(): east_rim[:, :, :, None]]
  transfers between devices with their start and end apart: 28 -> 7, of which waited for: 20 -> 2; matrix products, arithmetic and copies ran while one was open for 23% -> 0% of each run, Pallas kernels for 0% -> 22%
where the time goes in v1:
time: 25.2 us; the launch traced here: 25 us
  starting transfers between devices  11.3 us (45%)
  Pallas kernels  10.5 us (42%)
  waiting for transfers between devices  2.5 us (10%)
  between operations  0.68 us (3%)
    ppermute x4, starting transfers between devices, swapped(): return lax.ppermute(value, ('lat', 'lon'), pairs)  6.28 us
    pallas_call x1, Pallas kernels, shards(): call(functools.partial(wave_kernel, z, lat_count), (jax.ShapeDtypeStruct(...  5.19 us
    ppermute x3, starting transfers between devices, shifted(): lax.ppermute(value, axis, [(i, (i + steps) % count) for i in range(count)])  5.05 us
    pallas_call x1, Pallas kernels, shards(): call(functools.partial(sums_kernel, z), (whole, flat(z.sec_tiles), edge_r...  3.7 us
    ppermute x3, waiting for transfers between devices, shifted(): lax.ppermute(value, axis, [(i, (i + steps) % count) for i in range(count)])  2.48 us
    pallas_call x1, Pallas kernels, shards(): call(functools.partial(ocean_kernel, z, lat_count), (jax.ShapeDtypeStruct...  1.23 us
  transfers between devices with their start and end apart: 7, of which 2 were waited for; matrix products, arithmetic and copies ran while one was open for 0% of the time, Pallas kernels for 22%

profile of v1, /device:TPU:0, one launch (start us, length us, event | category | flops | bytes accessed | tf_op | source)
XLA Modules:
  0.0 25.0 jit_solution(6764308323849281415)
XLA Ops:
  0.6 3.7 %spectra_sums.1 = (f32[18,36,8,128]{3,2,1,0:T(8,128)S(1)}, f32[176,128]{1,0:T(8,128)S(1)}, f32[324,128]{1,0:T(8,128)S(1)}, f32[324,128]{1,0:T(8,128)S(1)}, f32[2...) custom-call(f32[18,36,8,128]{3,2,1,0:T(8,128)} %x.1, ...), custom_call_target="tpu_custom_call" | custom-call | flops 10616832 | bytes 2654208 | tf_op jit(solution)/shard_map/spectra_sums/pallas_call | solution.py:554
  4.3 3.0 %collective-permute-start = (f32[176,128]{1,0:T(8,128)S(1)}, f32[176,128]{1,0:T(8,128)S(1)}, u32[]{:S(2)}, u32[]{:S(2)}) collective-permute-start(f32[176,128]{1,0:T(8,128)S(1)} %get-tuple-element.23.mine), channel_id=1, source_target_pairs={{0,16},{16,0},{1,17},{17,1},{2,18},{18,2},{3,19},{19,3},{4,20},{20... | collective-permute-start | bytes 270344 | tf_op jit(solution)/shard_map/ppermute | solution.py:503
  7.3 1.6 %collective-permute-start.3 = (f32[324,128]{1,0:T(8,128)S(1)}, f32[324,128]{1,0:T(8,128)S(1)}, u32[]{:S(2)}, u32[]{:S(2)}) collective-permute-start(f32[324,128]{1,0:T(8,128)S(1)} %get-tuple-element.35), channel_id=1, source_target_pairs={{0,4},{1,5},{2,6},{3,7},{4,0},{5,1},{6,2},{7,3},{8,12},{9,13},{10,... | collective-permute-start | bytes 497672 | tf_op jit(solution)/shard_map/ppermute | solution.py:516
  8.9 1.0 %collective-permute-done.other = f32[176,128]{1,0:T(8,128)S(1)} collective-permute-done((f32[176,128]{1,0:T(8,128)S(1)}, f32[176,128]{1,0:T(8,128)S(1)}, u32[]{:S(2)}, u32[]{:S(2)}) %collective-permute-start) | collective-permute-done | bytes 90144 | tf_op jit(solution)/shard_map/ppermute | solution.py:503
  10.0 0.2 pack_columns.1
  10.1 0.1 collective-permute-start.4
  10.2 0.5 %collective-permute-start.1 = (f32[32,128]{1,0:T(8,128)S(1)}, f32[32,128]{1,0:T(8,128)S(1)}, u32[]{:S(2)}, u32[]{:S(2)}) collective-permute-start(f32[32,128]{1,0:T(8,128)S(1)} %get-tuple-element.29), channel_id=1, source_target_pairs={{0,1},{1,2},{2,3},{3,0},{4,5},{5,6},{6,7},{7,4},{8,9},{9,10},{10,1... | collective-permute-start | bytes 49160 | tf_op jit(solution)/shard_map/ppermute | solution.py:503
  10.7 1.5 %collective-permute-start.2 = (f32[32,128]{1,0:T(8,128)S(1)}, f32[32,128]{1,0:T(8,128)S(1)}, u32[]{:S(2)}, u32[]{:S(2)}) collective-permute-start(f32[32,128]{1,0:T(8,128)S(1)} %get-tuple-element.30), channel_id=1, source_target_pairs={{0,3},{1,0},{2,1},{3,2},{4,7},{5,4},{6,5},{7,6},{8,11},{9,8},{10,9... | collective-permute-start | bytes 49160 | tf_op jit(solution)/shard_map/ppermute | solution.py:503
  12.2 1.4 %collective-permute-done.1.from_west = f32[32,128]{1,0:T(8,128)S(1)} collective-permute-done((f32[32,128]{1,0:T(8,128)S(1)}, f32[32,128]{1,0:T(8,128)S(1)}, u32[]{:S(2)}, u32[]{:S(2)}) %collective-permute-start.1) | collective-permute-done | bytes 16416 | tf_op jit(solution)/shard_map/ppermute | solution.py:503
  13.7 0.0 collective-permute-done.2.from_east
  13.7 0.2 pack_rows.1
  13.9 3.3 %collective-permute-start.5 = (f32[112,128]{1,0:T(8,128)S(1)}, f32[112,128]{1,0:T(8,128)S(1)}, u32[]{:S(2)}, u32[]{:S(2)}) collective-permute-start(f32[112,128]{1,0:T(8,128)S(1)} %get-tuple-element.38), channel_id=1, source_target_pairs={{0,4},{1,5},{2,6},{3,7},{4,0},{5,1},{6,2},{7,3},{8,12},{9,13},{10,... | collective-permute-start | bytes 172040 | tf_op jit(solution)/shard_map/ppermute | solution.py:516
  17.2 1.3 %collective-permute-start.6 = (f32[112,128]{1,0:T(8,128)S(1)}, f32[112,128]{1,0:T(8,128)S(1)}, u32[]{:S(2)}, u32[]{:S(2)}) collective-permute-start(f32[112,128]{1,0:T(8,128)S(1)} %get-tuple-element.39), channel_id=1, source_target_pairs={{0,1},{1,0},{2,3},{3,2},{4,8},{5,9},{6,10},{7,11},{8,4},{9,5},{10,... | collective-permute-start | bytes 172040 | tf_op jit(solution)/shard_map/ppermute | solution.py:516
  18.5 0.0 collective-permute-done.3.first
  18.5 0.0 collective-permute-done.4.second
  18.5 5.2 %wave_step.1 = (f32[18,36,8,128]{3,2,1,0:T(8,128)}, f32[4,8,128]{2,1,0:T(8,128)S(1)}) custom-call(f32[18,36,8,128]{3,2,1,0:T(8,128)S(1)} %get-tuple-element.22.x, f32[16,8,128]{2,1,0:T(8,128)S(1)} %get-tuple-element.28.fields, f32[4,8,128]{2,1,0:T(8,128)S(1)} %get-tuple-element.33.coup, f32[16,128]{1,0:T(8,128)S(1)} %get-tuple-element.24.local, ...), custom_call_target="tpu_custom_call" | custom-call | flops 5971968 | bytes 5308416 | tf_op jit(solution)/shard_map/wave_step/pallas_call | solution.py:602
  23.7 0.0 collective-permute-done.5.from_first
  23.8 0.0 collective-permute-done.6.from_second
  23.8 1.2 %ocean_steps.1 = f32[2,4,8,128]{3,2,1,0:T(8,128)} custom-call(f32[112,128]{1,0:T(8,128)S(1)} %collective-permute-done.5.from_first, f32[112,128]{1,0:T(8,128)S(1)} %collective-permute-done.6.from_second, f32[16,8,128]{2,1,0:T(8,128)S(1)} %get-tuple-element.28.fields, f32[4,8,128]{2,1,0:T(8,128)S(1)} %get-tuple-element.40.coup, ...), custom_call_target="tpu_custom_call" | custom-call | flops 1048576 | bytes 1048576 | tf_op jit(solution)/shard_map/ocean_steps/pallas_call | solution.py:613
Async XLA Ops:
  4.3 5.6 %collective-permute-start = (f32[176,128]{1,0:T(8,128)S(1)}, f32[176,128]{1,0:T(8,128)S(1)}, u32[]{:S(2)}, u32[]{:S(2)}) collective-permute-start(f32[176,128]{1,0:T(8,128)S(1)} %get-tuple-element.23.mine), channel_id=1, source_target_pairs={{0,16},{16,0},{1,17},{17,1},{2,18},{18,2},{3,19},{19,3},{4,20},{20... | collective-permute-start | bytes 270344 | tf_op jit(solution)/shard_map/ppermute | solution.py:503
  7.3 11.2 %collective-permute-start.3 = (f32[324,128]{1,0:T(8,128)S(1)}, f32[324,128]{1,0:T(8,128)S(1)}, u32[]{:S(2)}, u32[]{:S(2)}) collective-permute-start(f32[324,128]{1,0:T(8,128)S(1)} %get-tuple-element.35), channel_id=1, source_target_pairs={{0,4},{1,5},{2,6},{3,7},{4,0},{5,1},{6,2},{7,3},{8,12},{9,13},{10,... | collective-permute-start | bytes 497672 | tf_op jit(solution)/shard_map/ppermute | solution.py:516
  10.1 8.4 %collective-permute-start.4 = (f32[324,128]{1,0:T(8,128)S(1)}, f32[324,128]{1,0:T(8,128)S(1)}, u32[]{:S(2)}, u32[]{:S(2)}) collective-permute-start(f32[324,128]{1,0:T(8,128)S(1)} %get-tuple-element.36), channel_id=1, source_target_pairs={{0,1},{1,0},{2,3},{3,2},{4,8},{5,9},{6,10},{7,11},{8,4},{9,5},{10,... | collective-permute-start | bytes 497672 | tf_op jit(solution)/shard_map/ppermute | solution.py:516
  10.2 3.5 %collective-permute-start.1 = (f32[32,128]{1,0:T(8,128)S(1)}, f32[32,128]{1,0:T(8,128)S(1)}, u32[]{:S(2)}, u32[]{:S(2)}) collective-permute-start(f32[32,128]{1,0:T(8,128)S(1)} %get-tuple-element.29), channel_id=1, source_target_pairs={{0,1},{1,2},{2,3},{3,0},{4,5},{5,6},{6,7},{7,4},{8,9},{9,10},{10,1... | collective-permute-start | bytes 49160 | tf_op jit(solution)/shard_map/ppermute | solution.py:503
  10.7 3.0 %collective-permute-start.2 = (f32[32,128]{1,0:T(8,128)S(1)}, f32[32,128]{1,0:T(8,128)S(1)}, u32[]{:S(2)}, u32[]{:S(2)}) collective-permute-start(f32[32,128]{1,0:T(8,128)S(1)} %get-tuple-element.30), channel_id=1, source_target_pairs={{0,3},{1,0},{2,1},{3,2},{4,7},{5,4},{6,5},{7,6},{8,11},{9,8},{10,9... | collective-permute-start | bytes 49160 | tf_op jit(solution)/shard_map/ppermute | solution.py:503
  13.9 9.8 %collective-permute-start.5 = (f32[112,128]{1,0:T(8,128)S(1)}, f32[112,128]{1,0:T(8,128)S(1)}, u32[]{:S(2)}, u32[]{:S(2)}) collective-permute-start(f32[112,128]{1,0:T(8,128)S(1)} %get-tuple-element.38), channel_id=1, source_target_pairs={{0,4},{1,5},{2,6},{3,7},{4,0},{5,1},{6,2},{7,3},{8,12},{9,13},{10,... | collective-permute-start | bytes 172040 | tf_op jit(solution)/shard_map/ppermute | solution.py:516
  17.2 6.5 %collective-permute-start.6 = (f32[112,128]{1,0:T(8,128)S(1)}, f32[112,128]{1,0:T(8,128)S(1)}, u32[]{:S(2)}, u32[]{:S(2)}) collective-permute-start(f32[112,128]{1,0:T(8,128)S(1)} %get-tuple-element.39), channel_id=1, source_target_pairs={{0,1},{1,0},{2,3},{3,2},{4,8},{5,9},{6,10},{7,11},{8,4},{9,5},{10,... | collective-permute-start | bytes 172040 | tf_op jit(solution)/shard_map/ppermute | solution.py:516

commit v2 on v1

--- a/solution.py
+++ b/solution.py
@@ -23,6 +23,7 @@
 SMEM = pl.BlockSpec(memory_space=pltpu.SMEM)
 ANY = pl.BlockSpec(memory_space=pl.ANY)
 F32 = jnp.float32
+BF16 = jnp.bfloat16
 
 
 def lanes():
@@ -111,9 +112,9 @@
     return result
 
 
-def sums_kernel(z, x, cur_in, mask_in, diffusion_in, courant_in, stokes_in, stress_in, table_in, buf, pay, first_rows, second_rows, ecol, wcol, local, coef, cur, mask, courant, stokes, stress, table, acc, sems, small_sems):
+def sums_kernel(z, x, cur_in, mask_in, diffusion_in, courant_in, stokes_in, stress_in, buf, pay, ecol, wcol, local, coef, cur, mask, courant, stokes, stress, acc, sems, small_sems):
     q, nf = z.quarter, z.freqs
-    pairs = ((cur_in, cur), (mask_in, mask), (diffusion_in, local.at[pl.ds(ROWS, ROWS)]), (courant_in, courant), (stokes_in, stokes), (stress_in, stress), (table_in, table))
+    pairs = ((cur_in, cur), (mask_in, mask), (diffusion_in, local.at[pl.ds(ROWS, ROWS)]), (courant_in, courant), (stokes_in, stokes), (stress_in, stress))
     small = [pltpu.make_async_copy(source, target, small_sems.at[k]) for k, (source, target) in enumerate(pairs)]
     for copy in small:
         copy.start()
@@ -128,9 +129,8 @@
     zero = jnp.zeros((ROWS, LANES), F32)
     for k in range(5 * SUMS):
         acc[k] = zero
-    for t in range(z.col_tiles):
-        put(ecol, t, zero)
-        put(wcol, t, zero)
+    sizes = tables(z.directions)
+    east, west = [zero] * z.col_tiles, [zero] * z.col_tiles
     for copy in small:
         copy.wait()
     sea = mask[...].astype(F32)
@@ -141,11 +141,10 @@
     for f in range(nf):
         coef[pl.ds(f, 1), :] = jnp.full((1, LANES), courant[f], F32)
 
-    def body(i, _):
-        c, s = table[0, i], table[1, i]
+    def add(i):
+        c, s = float(sizes[0, i]), float(sizes[1, i])
         heading = z.headings(i)
         total = [[zero] * 4 for _ in range(4)]
-        east, west = [zero] * z.col_tiles, [zero] * z.col_tiles
         for f in range(nf):
             t = f // z.per_tile
             cg = courant[f]
@@ -154,15 +153,11 @@
                 energy = buf[f, heading[j]]
                 for k in range(4):
                     total[k][j] = total[k][j] + factors[k] * energy
-                at = f % z.per_tile * z.half + (0 if j in (0, 1) else 1)
+                at = f % z.per_tile * z.half + 2 * i + (0 if j in (0, 1) else 1)
                 if j in (0, 3):
                     east[t] = jnp.where(lane == at, lane_roll(energy, at - (LANES - 1)), east[t])
                 else:
                     west[t] = jnp.where(lane == at, lane_roll(energy, at), west[t])
-        mine = lax.div(lax.rem(lane, z.half), 2) == i
-        for ref, tiles in ((ecol, east), (wcol, west)):
-            for t in range(z.col_tiles):
-                put(ref, t, jnp.where(mine, lane_roll(tiles[t], 2 * i), take(ref, t)))
         cc, cs, ss = c * c, c * s, s * s
         for w in range(2):
             plain, fast = total[2 * w], total[2 * w + 1]
@@ -191,19 +186,15 @@
                 for m in range(MOMENTS):
                     at = kind * SUMS + w * MOMENTS + m
                     acc[at] = acc[at] + values[kind * MOMENTS + m]
-        return 0
 
     for g, (lo, hi, _) in enumerate(chunks(z)):
         for copy in copies[4 * g : 4 * g + 4]:
             copy.wait()
-        lax.fori_loop(lo, hi, body, 0)
-
-    flat = buf.reshape(nf * z.directions * ROWS, LANES)
-    odd = lax.rem(lax.axis_index("lat"), 2)
-    north, south = ROWS - 1, z.half * ROWS
-    for ref, start in ((first_rows, north + odd * (south - north)), (second_rows, south + odd * (north - south))):
-        for f in range(nf):
-            ref[pl.ds(f * z.half, z.half), :] = flat[pl.ds(f * z.directions * ROWS + start, z.half, stride=ROWS), :]
+        for i in range(lo, hi):
+            add(i)
+    for t in range(z.col_tiles):
+        put(ecol, t, east[t])
+        put(wcol, t, west[t])
 
     cols = zero
     for k in range(SUMS):
@@ -221,7 +212,32 @@
         pay[pl.ds(z.sec_tiles * ROWS - spare, spare), :] = jnp.zeros((spare, LANES), F32)
 
 
-def columns_kernel(z, mine, other, local, ecol, wcol, second_rows, fields, coup, flux, to_east, to_west, second_out):
+def parts(tile):
+    high = tile.astype(BF16).astype(F32)
+    return high, (tile - high).astype(BF16).astype(F32)
+
+
+def edge_rows_kernel(z, x, first_rows, second_rows):
+    flat = x.reshape(z.freqs * z.directions * ROWS, LANES)
+    odd = lax.rem(lax.axis_index("lat"), 2)
+    north, south = ROWS - 1, z.half * ROWS
+    for ref, start in ((first_rows, north + odd * (south - north)), (second_rows, south + odd * (north - south))):
+        for f in range(z.freqs):
+            ref[pl.ds(f * z.half, z.half), :] = flat[pl.ds(f * z.directions * ROWS + start, z.half, stride=ROWS), :]
+
+
+def matrices_kernel(z, x, picks, beside):
+    lane = lanes()
+    for k in range(z.half // 2):
+        both = [((lane & (LANES // 2 - 1)) == 2 * k + n).astype(F32) for n in range(2)]
+        picks[pl.ds(2 * ROWS * k, 2 * ROWS), :] = jnp.concatenate(both, axis=0).astype(BF16)
+    shape = (2 * LANES, 2 * LANES)
+    apart = lax.broadcasted_iota(jnp.int32, shape, 0) - lax.broadcasted_iota(jnp.int32, shape, 1)
+    apart = apart & (2 * LANES - 1)
+    beside[...] = ((apart == 1) | (apart == 2 * LANES - 1)).astype(F32).astype(BF16)
+
+
+def columns_kernel(z, mine, other, picks, local, ecol, wcol, fields, coup, flux, to_east, to_west):
     lane, row = lanes(), rows()
     sec = lax.axis_index("sec")
     total = 2 * z.levels
@@ -259,7 +275,6 @@
     for t in range(z.col_tiles):
         put(to_east, 1 + t, take(ecol, t))
         put(to_west, 1 + t, take(wcol, t))
-    second_out[...] = second_rows[...]
 
 
 def rows_kernel(z, from_west, from_east, fields, coup, flux, local, coup_out, edges, to_first, to_second):
@@ -350,7 +365,7 @@
     return north, south
 
 
-def wave_kernel(z, lat_count, x, fields, coup, local, coef, from_west, from_east, first, second, out, coup_out, buf, scales, sides, sems):
+def wave_kernel(z, lat_count, x, fields, coup, local, coef, picks, from_west, from_east, first, second, out, coup_out, buf, scales, sides, sems):
     q, nf, half = z.quarter, z.freqs, z.half
     lane, row = lanes(), rows()
     total = 2 * z.levels
@@ -365,33 +380,42 @@
         c, s = float(sizes[0, i]), float(sizes[1, i])
         for j, heading in enumerate(z.headings(i)):
             sign_x, sign_y = side_signs(j)
-            headings.append((heading, c, s, sign_x, sign_y, 2 * i + (0 if j in (0, 1) else 1)))
+            headings.append((heading, i, sign_x, sign_y, 2 * i + (0 if j in (0, 1) else 1)))
             scales[heading] = sea * (1.0 + (sign_x * c) * zonal + (sign_y * s) * meridional)
+    ones = jnp.ones((LANES, LANES), BF16)
 
     def body(f, _):
         speed = spread(coef, f)
-        at = pl.ds(pl.multiple_of((1 + lax.div(f, z.per_tile)) * ROWS, ROWS), ROWS)
-        back = LANES - half * lax.rem(f, z.per_tile)
-        west, east = lane_roll(from_west[at, :], back), lane_roll(from_east[at, :], back)
-        for heading, c, s, sign_x, sign_y, k in headings:
+        along = [speed * float(sizes[0, i]) for i in range(q)]
+        across = [speed * float(sizes[1, i]) for i in range(q)]
+        stay = [1.0 - along[i] - across[i] for i in range(q)]
+        at = pl.ds(pl.multiple_of((1 + (f // z.per_tile)) * ROWS, ROWS), ROWS)
+        back = LANES - half * (f % z.per_tile)
+        rims = []
+        for ref in (from_west, from_east):
+            high, low = parts(lane_roll(ref[at, :], back))
+            both = jnp.where(lane < LANES // 2, high, lane_roll(low, LANES // 2))
+            both = jnp.concatenate([both, both], axis=0).astype(BF16)
+            chosen = jnp.concatenate([both] * (half // 2), axis=0) * picks[...]
+            rims.append(jnp.dot(chosen, ones, preferred_element_type=F32))
+        for heading, i, sign_x, sign_y, k in headings:
             energy = x[f, heading]
             if sign_x > 0:
-                beside = jnp.where(lane == 0, lane_roll(west, -k), lane_roll(energy, 1))
+                beside = jnp.where(lane == 0, rims[0][k * ROWS : (k + 1) * ROWS], lane_roll(energy, 1))
             else:
-                beside = jnp.where(lane == LANES - 1, lane_roll(east, LANES - 1 - k), lane_roll(energy, -1))
+                beside = jnp.where(lane == LANES - 1, rims[1][k * ROWS : (k + 1) * ROWS], lane_roll(energy, -1))
             if sign_y > 0:
                 below = jnp.where(row == 0, spread(sides.at[1], f * half + heading), row_roll(energy, 1))
             else:
                 below = jnp.where(row == ROWS - 1, spread(sides.at[0], f * half + heading - half), row_roll(energy, -1))
-            step = c * (beside - energy) + s * (below - energy)
-            buf[f, heading] = scales[heading] * (energy + speed * step)
+            buf[f, heading] = scales[heading] * (stay[i] * energy + along[i] * beside + across[i] * below)
         return 0
 
-    parts = 3 if nf % 3 == 0 else 1
+    count = 3 if nf % 3 == 0 else 1
     copies = []
-    for g in range(parts):
-        span = pl.ds(g * (nf // parts), nf // parts)
-        lax.fori_loop(g * (nf // parts), (g + 1) * (nf // parts), body, 0)
+    for g in range(count):
+        span = pl.ds(g * (nf // count), nf // count)
+        lax.fori_loop(g * (nf // count), (g + 1) * (nf // count), body, 0, unroll=6 if nf % 18 == 0 else 1)
         copy = pltpu.make_async_copy(buf.at[span], out.at[span], sems.at[g])
         copy.start()
         copies.append(copy)
@@ -399,7 +423,7 @@
         copy.wait()
 
 
-def ocean_kernel(z, lat_count, from_first, from_second, fields, coup, flux, edges, local, currents_out, ext, force):
+def ocean_kernel(z, lat_count, from_first, from_second, fields, coup, flux, edges, local, beside, currents_out, ext, force, still, mixed):
     total = 2 * z.levels
     row = rows()
     sec = lax.axis_index("sec")
@@ -454,32 +478,34 @@
     shape = (2 * ROWS, 2 * LANES)
     row_all = lax.broadcasted_iota(jnp.int32, shape, 0)
     row_all = jnp.where(row_all >= 2 * ROWS - HALO, row_all - 2 * ROWS, row_all) + lax.axis_index("lat") * ROWS
-    rot = sea_all * (0.05 + 0.1 * (row_all.astype(F32) + 0.5) / (lat_count * ROWS))
+    rot = sea_all * (0.05 + 0.1 * (row_all.astype(F32) + 0.5) * (1.0 / (lat_count * ROWS)))
     spin = sea_all * kappa
 
-    def level_of(p):
-        return p + sec * (total - 1 - 2 * p)
-
-    mixes, centers = [], []
+    def by_level(function, p):
+        return jnp.where(sec == 0, function(p), function(total - 1 - p)).astype(F32)
+
     for p in range(total):
-        level = level_of(p)
-        mixes.append(0.04 + 0.0125 * lax.rem(7 * level, 5).astype(F32))
-        decay = 1.0 / (1.0 + jnp.full(shape, level, jnp.int32).astype(F32))
-        gain = jnp.where(level == 0, stress_gain, 0.0)
+        mix, decay, gain = by_level(lambda level: 0.04 + 0.0125 * (7 * level % 5), p), by_level(lambda level: 1.0 / (1.0 + level), p), by_level(lambda level: stress_gain if level == 0 else 0.0, p)
         force[p] = rot * decay * coupling[1] + sea_all * gain * coupling[2]
         force[total + p] = sea_all * gain * coupling[3] - rot * decay * coupling[0]
+        mixed[p] = sea_all * mix
+        still[p] = sea_all * (1.0 - mix * (1 if p in (0, total - 1) else 2)) - 4.0 * spin
     for step in range(ITERS):
         needed = min(total, z.levels + ITERS - 1 - step)
+        every = [ext[comp * total + p] for comp in range(2) for p in range(needed)]
+        high, low = parts(jnp.concatenate(every, axis=0))
+        ring = jnp.dot(high.astype(BF16), beside[...], preferred_element_type=F32)
+        ring = ring + jnp.dot(low.astype(BF16), beside[...], preferred_element_type=F32)
         after = []
         for comp in range(2):
             for p in range(needed):
-                value = ext[comp * total + p]
-                ring = (pltpu.roll(value, 1, 1) + pltpu.roll(value, 2 * LANES - 1, 1)) + (pltpu.roll(value, 1, 0) + pltpu.roll(value, 2 * ROWS - 1, 0))
+                at = comp * needed + p
+                value = every[at]
+                around = ring[2 * ROWS * at : 2 * ROWS * (at + 1)] + (pltpu.roll(value, 1, 0) + pltpu.roll(value, 2 * ROWS - 1, 0))
                 near = [ext[comp * total + other] for other in (p - 1, p + 1) if 0 <= other < total]
-                column = near[0] - value if len(near) == 1 else near[0] + near[1] - 2.0 * value
-                turned = ext[(1 - comp) * total + p]
-                turned = rot * turned if comp == 0 else -(rot * turned)
-                after.append(sea_all * (value + mixes[p] * column) + spin * (ring - 4.0 * value) + turned + force[comp * total + p])
+                turned = rot * ext[(1 - comp) * total + p]
+                moved = still[p] * value + spin * around + mixed[p] * sum(near[1:], near[0]) + force[comp * total + p]
+                after.append(moved + turned if comp == 0 else moved - turned)
         if step < ITERS - 1:
             for comp in range(2):
                 for p in range(needed):
@@ -487,9 +513,8 @@
         else:
             for comp in range(2):
                 for level in range(z.levels):
-                    own = level
                     place = level + sec * (z.levels - 1 - 2 * level)
-                    currents_out[comp, place] = after[comp * needed + own][:ROWS, :LANES]
+                    currents_out[comp, place] = after[comp * needed + level][:ROWS, :LANES]
 
 
 def tables(directions):
@@ -543,47 +568,71 @@
     lat_count = lax.axis_size("lat")
     assert lax.axis_size("sec") == 2 and (tile_rows, tile_cols) == (ROWS, LANES) and directions % 4 == 0
     z = Sizes(freqs, directions, levels)
-    table = jnp.asarray(tables(directions))
     size = spectra.size * 4
     copies = 4 * len(chunks(z))
     sems = pltpu.SemaphoreType.DMA((copies,))
     whole = pltpu.VMEM(spectra.shape, F32)
 
     edge_rows = jax.ShapeDtypeStruct((z.edge_rows, LANES), F32)
-    inputs = (spectra, currents, land_mask, diffusion, courant, stokes_weight, stress_weight, table)
-    kept, pay, first_rows, second_rows, ecol, wcol, local, coef = call(
+    inputs = (spectra, currents, land_mask, diffusion, courant, stokes_weight, stress_weight)
+    kept, pay, ecol, wcol, local, coef = call(
         functools.partial(sums_kernel, z),
-        (whole, flat(z.sec_tiles), edge_rows, edge_rows, flat(z.col_tiles), flat(z.col_tiles), flat(2), flat(z.coef_tiles)),
-        [ANY] * 8,
+        (
+            whole,
+            flat(z.sec_tiles),
+            flat(z.col_tiles),
+            flat(z.col_tiles),
+            flat(2),
+            flat(z.coef_tiles),
+        ),
+        [ANY] * 7,
         scratch=[
             pltpu.VMEM(currents.shape, F32),
             pltpu.VMEM(land_mask.shape, jnp.int32),
             pltpu.SMEM(courant.shape, F32),
             pltpu.SMEM(courant.shape, F32),
             pltpu.SMEM(courant.shape, F32),
-            pltpu.SMEM(table.shape, F32),
             pltpu.VMEM((5 * SUMS, ROWS, LANES), F32),
             sems,
-            pltpu.SemaphoreType.DMA((7,)),
+            pltpu.SemaphoreType.DMA((6,)),
         ],
         name="spectra_sums",
         bytes_accessed=size,
         flops=16 * size // 4,
     )(*[pltpu.with_memory_space_constraint(array, pltpu.HBM) for array in inputs])
 
+    other = shifted(pay, "sec", 1)
+
+    first_rows, second_rows = call(
+        functools.partial(edge_rows_kernel, z),
+        (edge_rows, edge_rows),
+        [VMEM],
+        name="pick_rows",
+        bytes_accessed=size,
+        flops=8 * size // 4,
+    )(kept)
+
     got_first = swapped(first_rows, 0)
-    other = shifted(pay, "sec", 1)
-
-    fields, coup, flux, to_east, to_west, second_rows = call(
+    got_second = swapped(second_rows, 1)
+
+    picks, beside = call(
+        functools.partial(matrices_kernel, z),
+        (jax.ShapeDtypeStruct((z.half * ROWS, LANES), BF16), jax.ShapeDtypeStruct((2 * LANES, 2 * LANES), BF16)),
+        [VMEM],
+        name="matrices",
+        bytes_accessed=size,
+        flops=8388608,
+    )(kept)
+
+    fields, coup, flux, to_east, to_west = call(
         functools.partial(columns_kernel, z),
-        (stack(z.fields), stack(4), flat(1 + z.sec_tiles - z.sec_rows), flat(1 + z.col_tiles), flat(1 + z.col_tiles), edge_rows),
+        (stack(z.fields), stack(4), flat(1 + z.sec_tiles - z.sec_rows), flat(1 + z.col_tiles), flat(1 + z.col_tiles)),
         [VMEM] * 6,
         name="pack_columns",
         bytes_accessed=2**18,
-        flops=2**16,
-    )(pay, other, local, ecol, wcol, second_rows)
-
-    got_second = swapped(second_rows, 1)
+        flops=65536,
+    )(pay, other, picks, local, ecol, wcol)
+
     from_east = shifted(to_west, "lon", -1)
     from_west = shifted(to_east, "lon", 1)
 
@@ -593,7 +642,7 @@
         [VMEM] * 6,
         name="pack_rows",
         bytes_accessed=2**18,
-        flops=2**16,
+        flops=2**27,
     )(from_west, from_east, fields, coup, flux, local)
 
     from_second = swapped(to_second, 1)
@@ -602,23 +651,23 @@
     new_spectra, coup = call(
         functools.partial(wave_kernel, z, lat_count),
         (jax.ShapeDtypeStruct(spectra.shape, F32), stack(4)),
-        [VMEM] * 9,
+        [VMEM] * 10,
         out_specs=[ANY, VMEM],
         scratch=[whole, pltpu.VMEM((directions, ROWS, LANES), F32), pltpu.VMEM((2, z.edge_rows, LANES), F32), sems],
         name="wave_step",
         bytes_accessed=2 * size,
-        flops=9 * size // 4,
-    )(kept, fields, coup, local, coef, from_west, from_east, got_first, got_second)
+        flops=8388608,
+    )(kept, fields, coup, local, coef, picks, from_west, from_east, got_first, got_second)
 
     (new_currents,) = call(
         functools.partial(ocean_kernel, z, lat_count),
         (jax.ShapeDtypeStruct(currents.shape, F32),),
-        [VMEM] * 7,
-        scratch=[pltpu.VMEM((z.fields, 2 * ROWS, 2 * LANES), F32), pltpu.VMEM((z.fields, 2 * ROWS, 2 * LANES), F32)],
+        [VMEM] * 8,
+        scratch=[pltpu.VMEM((count, 2 * ROWS, 2 * LANES), F32) for count in (z.fields, z.fields, 2 * levels, 2 * levels)],
         name="ocean_steps",
         bytes_accessed=2**20,
         flops=2**20,
-    )(from_first, from_second, fields, coup, flux, edges, local)
+    )(from_first, from_second, fields, coup, flux, edges, local, beside)
     return new_spectra, new_currents
 
 

time: 25.2 us -> 20.7 us (0.82)
  Pallas kernels: 10.5 us -> 7.41 us
  starting transfers between devices: 11.3 us -> 10.1 us
    pallas_call x1, Pallas kernels: 5.19 us -> 2.67 us  [shards(): call(functools.partial(wave_kernel, z, lat_count), (jax.ShapeDtypeStruct(...]
    ppermute x4, starting transfers between devices: 6.28 us -> 5.34 us  [swapped(): return lax.ppermute(value, ('lat', 'lon'), pairs)]
    pallas_call x1 -> x3, Pallas kernels: 3.7 us -> 2.83 us  [the longest x1 2.7 us: shards(): call(functools.partial(sums_kernel, z), (whole, flat(z.sec_tiles), flat(z...]
    pallas_call x1, Pallas kernels: 1.23 us -> 1.53 us  [shards(): call(functools.partial(ocean_kernel, z, lat_count), (jax.ShapeDtypeStruct...]
  transfers between devices with their start and end apart: 7 -> 7, of which waited for: 2 -> 2; matrix products, arithmetic and copies ran while one was open for 0% -> 0% of each run, Pallas kernels for 22% -> 16%
where the time goes in v2:
time: 20.7 us; the launch traced here: 20.5 us
  starting transfers between devices  10.1 us (49%)
  Pallas kernels  7.41 us (36%)
  waiting for transfers between devices  2.29 us (11%)
  between operations  0.69 us (3%)
    ppermute x4, starting transfers between devices, swapped(): return lax.ppermute(value, ('lat', 'lon'), pairs)  5.34 us
    ppermute x3, starting transfers between devices, shifted(): lax.ppermute(value, axis, [(i, (i + steps) % count) for i in range(count)])  4.79 us
    pallas_call x1, Pallas kernels, shards(): call(functools.partial(sums_kernel, z), (whole, flat(z.sec_tiles), flat(z...  2.7 us
    pallas_call x1, Pallas kernels, shards(): call(functools.partial(wave_kernel, z, lat_count), (jax.ShapeDtypeStruct(...  2.67 us
    ppermute x3, waiting for transfers between devices, shifted(): lax.ppermute(value, axis, [(i, (i + steps) % count) for i in range(count)])  2.28 us
    pallas_call x1, Pallas kernels, shards(): call(functools.partial(ocean_kernel, z, lat_count), (jax.ShapeDtypeStruct...  1.53 us
  transfers between devices with their start and end apart: 7, of which 2 were waited for; matrix products, arithmetic and copies ran while one was open for 0% of the time, Pallas kernels for 16%

profile of v2, /device:TPU:0, one launch (start us, length us, event | category | flops | bytes accessed | tf_op | source)
XLA Modules:
  0.0 20.5 jit_solution(16759588559172103275)
XLA Ops:
  0.6 2.7 %spectra_sums.1 = (f32[18,36,8,128]{3,2,1,0:T(8,128)S(1)}, f32[176,128]{1,0:T(8,128)S(1)}, f32[24,128]{1,0:T(8,128)S(1)}, f32[24,128]{1,0:T(8,128)S(1)}, f32[16,128]{1,0:T(8,128)S(1)}, /*index=5*/f32[24,128]{1,0:T(8,128)S(1)}) custom-call(f32[18,36,8,128]{3,2,1,0:T(8,128)} %x.1, f32[2,4,8,128]{3,2,1,0:T(8,128)} %cur_in.1, s32[8,128]{1,0:T(8,128)} %mask_in.1, ...), custom_call_target="tpu_custom_call" | custom-call | flops 10616832 | bytes 2654208 | tf_op jit(solution)/shard_map/spectra_sums/pallas_call | solution.py:578
  3.3 3.0 %collective-permute-start = (f32[176,128]{1,0:T(8,128)S(1)}, f32[176,128]{1,0:T(8,128)S(1)}, u32[]{:S(2)}, u32[]{:S(2)}) collective-permute-start(f32[176,128]{1,0:T(8,128)S(1)} %get-tuple-element.24.mine), channel_id=1, source_target_pairs={{0,16},{16,0},{1,17},{17,1},{2,18},{18,2},{3,19},{19,3},{4,20},{20... | collective-permute-start | bytes 270344 | tf_op jit(solution)/shard_map/ppermute | solution.py:528
  6.3 0.1 pick_rows.1
  6.4 1.6 %collective-permute-start.3 = (f32[324,128]{1,0:T(8,128)S(1)}, f32[324,128]{1,0:T(8,128)S(1)}, u32[]{:S(2)}, u32[]{:S(2)}) collective-permute-start(f32[324,128]{1,0:T(8,128)S(1)} %get-tuple-element.36), channel_id=1, source_target_pairs={{0,4},{1,5},{2,6},{3,7},{4,0},{5,1},{6,2},{7,3},{8,12},{9,13},{10,... | collective-permute-start | bytes 497672 | tf_op jit(solution)/shard_map/ppermute | solution.py:541
  8.1 0.0 collective-permute-start.4
  8.1 0.8 %collective-permute-done.other = f32[176,128]{1,0:T(8,128)S(1)} collective-permute-done((f32[176,128]{1,0:T(8,128)S(1)}, f32[176,128]{1,0:T(8,128)S(1)}, u32[]{:S(2)}, u32[]{:S(2)}) %collective-permute-start) | collective-permute-done | bytes 90144 | tf_op jit(solution)/shard_map/ppermute | solution.py:528
  9.0 0.2 pack_columns.1
  9.1 0.1 collective-permute-start.1
  9.2 1.7 %collective-permute-start.2 = (f32[32,128]{1,0:T(8,128)S(1)}, f32[32,128]{1,0:T(8,128)S(1)}, u32[]{:S(2)}, u32[]{:S(2)}) collective-permute-start(f32[32,128]{1,0:T(8,128)S(1)} %get-tuple-element.31), channel_id=1, source_target_pairs={{0,3},{1,0},{2,1},{3,2},{4,7},{5,4},{6,5},{7,6},{8,11},{9,8},{10,9... | collective-permute-start | bytes 49160 | tf_op jit(solution)/shard_map/ppermute | solution.py:528
  10.9 1.4 %collective-permute-done.1.from_west = f32[32,128]{1,0:T(8,128)S(1)} collective-permute-done((f32[32,128]{1,0:T(8,128)S(1)}, f32[32,128]{1,0:T(8,128)S(1)}, u32[]{:S(2)}, u32[]{:S(2)}) %collective-permute-start.1) | collective-permute-done | bytes 16416 | tf_op jit(solution)/shard_map/ppermute | solution.py:528
  12.3 0.0 collective-permute-done.2.from_east
  12.4 0.2 %pack_rows.1 = (f32[4,8,128]{2,1,0:T(8,128)S(1)}, f32[32,8,128]{2,1,0:T(8,128)S(1)}, f32[112,128]{1,0:T(8,128)S(1)}, f32[112,128]{1,0:T(8,128)S(1)}) custom-call(f32[32,128]{1,0:T(8,128)S(1)} %collective-permute-done.1.from_west, f32[32,128]{1,0:T(8,128)S(1)} %collective-permute-done.2.from_east, f32[16,8,128]{2,1,0:T(8,128)S(1)} %get-tuple-element.29.fields, ...), custom_call_target="tpu_custom_call" | custom-call | flops 134217728 | bytes 262144 | tf_op jit(solution)/shard_map/pack_rows/pallas_call | solution.py:639
  12.6 2.4 %collective-permute-start.5 = (f32[112,128]{1,0:T(8,128)S(1)}, f32[112,128]{1,0:T(8,128)S(1)}, u32[]{:S(2)}, u32[]{:S(2)}) collective-permute-start(f32[112,128]{1,0:T(8,128)S(1)} %get-tuple-element.39), channel_id=1, source_target_pairs={{0,4},{1,5},{2,6},{3,7},{4,0},{5,1},{6,2},{7,3},{8,12},{9,13},{10,... | collective-permute-start | bytes 172040 | tf_op jit(solution)/shard_map/ppermute | solution.py:541
  15.0 1.3 %collective-permute-start.6 = (f32[112,128]{1,0:T(8,128)S(1)}, f32[112,128]{1,0:T(8,128)S(1)}, u32[]{:S(2)}, u32[]{:S(2)}) collective-permute-start(f32[112,128]{1,0:T(8,128)S(1)} %get-tuple-element.40), channel_id=1, source_target_pairs={{0,1},{1,0},{2,3},{3,2},{4,8},{5,9},{6,10},{7,11},{8,4},{9,5},{10,... | collective-permute-start | bytes 172040 | tf_op jit(solution)/shard_map/ppermute | solution.py:541
  16.3 0.0 collective-permute-done.3.first
  16.3 0.0 collective-permute-done.4.second
  16.3 2.7 %wave_step.1 = (f32[18,36,8,128]{3,2,1,0:T(8,128)}, f32[4,8,128]{2,1,0:T(8,128)S(1)}) custom-call(f32[18,36,8,128]{3,2,1,0:T(8,128)S(1)} %get-tuple-element.23.x, f32[16,8,128]{2,1,0:T(8,128)S(1)} %get-tuple-element.29.fields, f32[4,8,128]{2,1,0:T(8,128)S(1)} %get-tuple-element.34.coup, f32[16,128]{1,0:T(8,128)S(1)} %get-tuple-element.26.local, ...), custom_call_target="tpu_custom_call" | custom-call | flops 8388608 | bytes 5308416 | tf_op jit(solution)/shard_map/wave_step/pallas_call | solution.py:651
  19.0 0.0 collective-permute-done.5.from_first
  19.0 0.0 collective-permute-done.6.from_second
  19.0 1.5 %ocean_steps.1 = f32[2,4,8,128]{3,2,1,0:T(8,128)} custom-call(f32[112,128]{1,0:T(8,128)S(1)} %collective-permute-done.5.from_first, f32[112,128]{1,0:T(8,128)S(1)} %collective-permute-done.6.from_second, f32[16,8,128]{2,1,0:T(8,128)S(1)} %get-tuple-element.29.fields, f32[4,8,128]{2,1,0:T(8,128)S(1)} %get-tuple-element.41.coup, ...), custom_call_target="tpu_custom_call" | custom-call | flops 1048576 | bytes 1048576 | tf_op jit(solution)/shard_map/ocean_steps/pallas_call | solution.py:662
  (1 shorter events, 0.0 us)
Async XLA Ops:
  3.3 5.6 %collective-permute-start = (f32[176,128]{1,0:T(8,128)S(1)}, f32[176,128]{1,0:T(8,128)S(1)}, u32[]{:S(2)}, u32[]{:S(2)}) collective-permute-start(f32[176,128]{1,0:T(8,128)S(1)} %get-tuple-element.24.mine), channel_id=1, source_target_pairs={{0,16},{16,0},{1,17},{17,1},{2,18},{18,2},{3,19},{19,3},{4,20},{20... | collective-permute-start | bytes 270344 | tf_op jit(solution)/shard_map/ppermute | solution.py:528
  6.4 9.9 %collective-permute-start.3 = (f32[324,128]{1,0:T(8,128)S(1)}, f32[324,128]{1,0:T(8,128)S(1)}, u32[]{:S(2)}, u32[]{:S(2)}) collective-permute-start(f32[324,128]{1,0:T(8,128)S(1)} %get-tuple-element.36), channel_id=1, source_target_pairs={{0,4},{1,5},{2,6},{3,7},{4,0},{5,1},{6,2},{7,3},{8,12},{9,13},{10,... | collective-permute-start | bytes 497672 | tf_op jit(solution)/shard_map/ppermute | solution.py:541
  8.1 8.2 %collective-permute-start.4 = (f32[324,128]{1,0:T(8,128)S(1)}, f32[324,128]{1,0:T(8,128)S(1)}, u32[]{:S(2)}, u32[]{:S(2)}) collective-permute-start(f32[324,128]{1,0:T(8,128)S(1)} %get-tuple-element.37), channel_id=1, source_target_pairs={{0,1},{1,0},{2,3},{3,2},{4,8},{5,9},{6,10},{7,11},{8,4},{9,5},{10,... | collective-permute-start | bytes 497672 | tf_op jit(solution)/shard_map/ppermute | solution.py:541
  9.1 3.2 %collective-permute-start.1 = (f32[32,128]{1,0:T(8,128)S(1)}, f32[32,128]{1,0:T(8,128)S(1)}, u32[]{:S(2)}, u32[]{:S(2)}) collective-permute-start(f32[32,128]{1,0:T(8,128)S(1)} %get-tuple-element.30), channel_id=1, source_target_pairs={{0,1},{1,2},{2,3},{3,0},{4,5},{5,6},{6,7},{7,4},{8,9},{9,10},{10,1... | collective-permute-start | bytes 49160 | tf_op jit(solution)/shard_map/ppermute | solution.py:528
  9.2 3.2 %collective-permute-start.2 = (f32[32,128]{1,0:T(8,128)S(1)}, f32[32,128]{1,0:T(8,128)S(1)}, u32[]{:S(2)}, u32[]{:S(2)}) collective-permute-start(f32[32,128]{1,0:T(8,128)S(1)} %get-tuple-element.31), channel_id=1, source_target_pairs={{0,3},{1,0},{2,1},{3,2},{4,7},{5,4},{6,5},{7,6},{8,11},{9,8},{10,9... | collective-permute-start | bytes 49160 | tf_op jit(solution)/shard_map/ppermute | solution.py:528
  12.6 6.4 %collective-permute-start.5 = (f32[112,128]{1,0:T(8,128)S(1)}, f32[112,128]{1,0:T(8,128)S(1)}, u32[]{:S(2)}, u32[]{:S(2)}) collective-permute-start(f32[112,128]{1,0:T(8,128)S(1)} %get-tuple-element.39), channel_id=1, source_target_pairs={{0,4},{1,5},{2,6},{3,7},{4,0},{5,1},{6,2},{7,3},{8,12},{9,13},{10,... | collective-permute-start | bytes 172040 | tf_op jit(solution)/shard_map/ppermute | solution.py:541
  15.0 4.0 %collective-permute-start.6 = (f32[112,128]{1,0:T(8,128)S(1)}, f32[112,128]{1,0:T(8,128)S(1)}, u32[]{:S(2)}, u32[]{:S(2)}) collective-permute-start(f32[112,128]{1,0:T(8,128)S(1)} %get-tuple-element.40), channel_id=1, source_target_pairs={{0,1},{1,0},{2,3},{3,2},{4,8},{5,9},{6,10},{7,11},{8,4},{9,5},{10,... | collective-permute-start | bytes 172040 | tf_op jit(solution)/shard_map/ppermute | solution.py:541

commit v3 on v2

--- a/solution.py
+++ b/solution.py
@@ -104,11 +104,11 @@
 
 def chunks(z):
     q = z.quarter
-    group = 3 if q % 3 == 0 else 1
+    cuts = sorted({0, q * 4 // 9, q * 7 // 9, q})
     result = []
-    for lo in range(0, q, group):
-        hi = lo + group
-        result.append((lo, hi, [pl.ds(start, group) for start in (lo, 2 * q - hi, 2 * q + lo, 4 * q - hi)]))
+    for lo, hi in zip(cuts, cuts[1:]):
+        starts = (lo, 2 * q - hi, 2 * q + lo, 4 * q - hi)
+        result.append((lo, hi, [pl.ds(start, hi - lo) for start in starts]))
     return result
 
 
@@ -217,24 +217,19 @@
     return high, (tile - high).astype(BF16).astype(F32)
 
 
-def edge_rows_kernel(z, x, first_rows, second_rows):
+def edge_rows_kernel(z, turn, x, out):
     flat = x.reshape(z.freqs * z.directions * ROWS, LANES)
-    odd = lax.rem(lax.axis_index("lat"), 2)
     north, south = ROWS - 1, z.half * ROWS
-    for ref, start in ((first_rows, north + odd * (south - north)), (second_rows, south + odd * (north - south))):
-        for f in range(z.freqs):
-            ref[pl.ds(f * z.half, z.half), :] = flat[pl.ds(f * z.directions * ROWS + start, z.half, stride=ROWS), :]
-
-
-def matrices_kernel(z, x, picks, beside):
+    start = jnp.where(lax.rem(lax.axis_index("lat"), 2) == turn, north, south)
+    for f in range(z.freqs):
+        out[pl.ds(f * z.half, z.half), :] = flat[pl.ds(f * z.directions * ROWS + start, z.half, stride=ROWS), :]
+
+
+def picks_kernel(z, x, picks):
     lane = lanes()
     for k in range(z.half // 2):
         both = [((lane & (LANES // 2 - 1)) == 2 * k + n).astype(F32) for n in range(2)]
         picks[pl.ds(2 * ROWS * k, 2 * ROWS), :] = jnp.concatenate(both, axis=0).astype(BF16)
-    shape = (2 * LANES, 2 * LANES)
-    apart = lax.broadcasted_iota(jnp.int32, shape, 0) - lax.broadcasted_iota(jnp.int32, shape, 1)
-    apart = apart & (2 * LANES - 1)
-    beside[...] = ((apart == 1) | (apart == 2 * LANES - 1)).astype(F32).astype(BF16)
 
 
 def columns_kernel(z, mine, other, picks, local, ecol, wcol, fields, coup, flux, to_east, to_west):
@@ -277,7 +272,7 @@
         put(to_west, 1 + t, take(wcol, t))
 
 
-def rows_kernel(z, from_west, from_east, fields, coup, flux, local, coup_out, edges, to_first, to_second):
+def rows_kernel(z, from_east, from_west, fields, coup, flux, local, got_rows, coup_out, edges, to_first, to_second):
     lane, row = lanes(), rows()
     total = 2 * z.levels
     top = lax.axis_index("sec") * (total - 1)
@@ -411,11 +406,11 @@
             buf[f, heading] = scales[heading] * (stay[i] * energy + along[i] * beside + across[i] * below)
         return 0
 
-    count = 3 if nf % 3 == 0 else 1
+    count = 6 if nf % 6 == 0 else 1
     copies = []
     for g in range(count):
         span = pl.ds(g * (nf // count), nf // count)
-        lax.fori_loop(g * (nf // count), (g + 1) * (nf // count), body, 0, unroll=6 if nf % 18 == 0 else 1)
+        lax.fori_loop(g * (nf // count), (g + 1) * (nf // count), body, 0, unroll=3 if nf % 18 == 0 else 1)
         copy = pltpu.make_async_copy(buf.at[span], out.at[span], sems.at[g])
         copy.start()
         copies.append(copy)
@@ -423,7 +418,7 @@
         copy.wait()
 
 
-def ocean_kernel(z, lat_count, from_first, from_second, fields, coup, flux, edges, local, beside, currents_out, ext, force, still, mixed):
+def ocean_kernel(z, lat_count, from_first, from_second, fields, coup, flux, edges, local, currents_out, ext, force, still, mixed):
     total = 2 * z.levels
     row = rows()
     sec = lax.axis_index("sec")
@@ -493,15 +488,12 @@
     for step in range(ITERS):
         needed = min(total, z.levels + ITERS - 1 - step)
         every = [ext[comp * total + p] for comp in range(2) for p in range(needed)]
-        high, low = parts(jnp.concatenate(every, axis=0))
-        ring = jnp.dot(high.astype(BF16), beside[...], preferred_element_type=F32)
-        ring = ring + jnp.dot(low.astype(BF16), beside[...], preferred_element_type=F32)
         after = []
         for comp in range(2):
             for p in range(needed):
                 at = comp * needed + p
                 value = every[at]
-                around = ring[2 * ROWS * at : 2 * ROWS * (at + 1)] + (pltpu.roll(value, 1, 0) + pltpu.roll(value, 2 * ROWS - 1, 0))
+                around = (pltpu.roll(value, 1, 1) + pltpu.roll(value, 2 * LANES - 1, 1)) + (pltpu.roll(value, 1, 0) + pltpu.roll(value, 2 * ROWS - 1, 0))
                 near = [ext[comp * total + other] for other in (p - 1, p + 1) if 0 <= other < total]
                 turned = rot * ext[(1 - comp) * total + p]
                 moved = still[p] * value + spin * around + mixed[p] * sum(near[1:], near[0]) + force[comp * total + p]
@@ -603,23 +595,26 @@
 
     other = shifted(pay, "sec", 1)
 
-    first_rows, second_rows = call(
-        functools.partial(edge_rows_kernel, z),
-        (edge_rows, edge_rows),
+    got_first, got_second = [
+        swapped(
+            call(
+                functools.partial(edge_rows_kernel, z, turn),
+                (edge_rows,),
+                [VMEM],
+                name="pick_rows",
+                bytes_accessed=size // 16,
+                flops=2**16,
+            )(kept)[0],
+            turn,
+        )
+        for turn in range(2)
+    ]
+
+    (picks,) = call(
+        functools.partial(picks_kernel, z),
+        (jax.ShapeDtypeStruct((z.half * ROWS, LANES), BF16),),
         [VMEM],
-        name="pick_rows",
-        bytes_accessed=size,
-        flops=8 * size // 4,
-    )(kept)
-
-    got_first = swapped(first_rows, 0)
-    got_second = swapped(second_rows, 1)
-
-    picks, beside = call(
-        functools.partial(matrices_kernel, z),
-        (jax.ShapeDtypeStruct((z.half * ROWS, LANES), BF16), jax.ShapeDtypeStruct((2 * LANES, 2 * LANES), BF16)),
-        [VMEM],
-        name="matrices",
+        name="picks",
         bytes_accessed=size,
         flops=8388608,
     )(kept)
@@ -630,7 +625,7 @@
         [VMEM] * 6,
         name="pack_columns",
         bytes_accessed=2**18,
-        flops=65536,
+        flops=1073741824,
     )(pay, other, picks, local, ecol, wcol)
 
     from_east = shifted(to_west, "lon", -1)
@@ -639,11 +634,11 @@
     coup, edges, to_first, to_second = call(
         functools.partial(rows_kernel, z),
         (stack(4), stack(z.arrays + SUMS), flat(z.lat_tiles), flat(z.lat_tiles)),
-        [VMEM] * 6,
+        [VMEM] * 7,
         name="pack_rows",
         bytes_accessed=2**18,
         flops=2**27,
-    )(from_west, from_east, fields, coup, flux, local)
+    )(from_east, from_west, fields, coup, flux, local, got_second)
 
     from_second = swapped(to_second, 1)
     from_first = swapped(to_first, 0)
@@ -656,18 +651,18 @@
         scratch=[whole, pltpu.VMEM((directions, ROWS, LANES), F32), pltpu.VMEM((2, z.edge_rows, LANES), F32), sems],
         name="wave_step",
         bytes_accessed=2 * size,
-        flops=8388608,
+        flops=9 * size // 4,
     )(kept, fields, coup, local, coef, picks, from_west, from_east, got_first, got_second)
 
     (new_currents,) = call(
         functools.partial(ocean_kernel, z, lat_count),
         (jax.ShapeDtypeStruct(currents.shape, F32),),
-        [VMEM] * 8,
+        [VMEM] * 7,
         scratch=[pltpu.VMEM((count, 2 * ROWS, 2 * LANES), F32) for count in (z.fields, z.fields, 2 * levels, 2 * levels)],
         name="ocean_steps",
         bytes_accessed=2**20,
         flops=2**20,
-    )(from_first, from_second, fields, coup, flux, edges, local, beside)
+    )(from_first, from_second, fields, coup, flux, edges, local)
     return new_spectra, new_currents
 
 

time: 20.7 us -> 19.1 us (0.923)
  starting transfers between devices: 10.1 us -> 8.04 us
  waiting for transfers between devices: 2.29 us -> 3.37 us
  Pallas kernels: 7.41 us -> 6.88 us
    ppermute x3, starting transfers between devices: 4.79 us -> 3.57 us  [shifted(): lax.ppermute(value, axis, [(i, (i + steps) % count) for i in range(count)])]
    ppermute x4, starting transfers between devices: 5.34 us -> 4.47 us  [swapped(): return lax.ppermute(value, ('lat', 'lon'), pairs)]
    ppermute x3, waiting for transfers between devices: 2.28 us -> 2.91 us  [shifted(): lax.ppermute(value, axis, [(i, (i + steps) % count) for i in range(count)])]
    ppermute x4, waiting for transfers between devices: 0.01 us -> 0.47 us  [swapped(): return lax.ppermute(value, ('lat', 'lon'), pairs)]
    pallas_call x1, Pallas kernels: 1.53 us -> 1.15 us  [shards(): call(functools.partial(ocean_kernel, z, lat_count), (jax.ShapeDtypeStruct...]
  transfers between devices with their start and end apart: 7 -> 7, of which waited for: 2 -> 3; matrix products, arithmetic and copies ran while one was open for 0% -> 0% of each run, Pallas kernels for 16% -> 16%
where the time goes in v3:
time: 19.1 us; the launch traced here: 19 us
  starting transfers between devices  8.04 us (42%)
  Pallas kernels  6.88 us (36%)
  waiting for transfers between devices  3.37 us (18%)
  between operations  0.69 us (4%)
    ppermute x4, starting transfers between devices, swapped(): return lax.ppermute(value, ('lat', 'lon'), pairs)  4.47 us
    ppermute x3, starting transfers between devices, shifted(): lax.ppermute(value, axis, [(i, (i + steps) % count) for i in range(count)])  3.57 us
    ppermute x3, waiting for transfers between devices, shifted(): lax.ppermute(value, axis, [(i, (i + steps) % count) for i in range(count)])  2.91 us
    pallas_call x1, Pallas kernels, shards(): call(functools.partial(sums_kernel, z), (whole, flat(z.sec_tiles), flat(z...  2.7 us
    pallas_call x1, Pallas kernels, shards(): call(functools.partial(wave_kernel, z, lat_count), (jax.ShapeDtypeStruct(...  2.52 us
    pallas_call x1, Pallas kernels, shards(): call(functools.partial(ocean_kernel, z, lat_count), (jax.ShapeDtypeStruct...  1.15 us
    ppermute x4, waiting for transfers between devices, swapped(): return lax.ppermute(value, ('lat', 'lon'), pairs)  0.47 us
  transfers between devices with their start and end apart: 7, of which 3 were waited for; matrix products, arithmetic and copies ran while one was open for 0% of the time, Pallas kernels for 16%

profile of v3, /device:TPU:0, one launch (start us, length us, event | category | flops | bytes accessed | tf_op | source)
XLA Modules:
  0.0 19.0 jit_solution(17160163769736276872)
XLA Ops:
  0.6 2.7 %spectra_sums.1 = (f32[18,36,8,128]{3,2,1,0:T(8,128)S(1)}, f32[176,128]{1,0:T(8,128)S(1)}, f32[24,128]{1,0:T(8,128)S(1)}, f32[24,128]{1,0:T(8,128)S(1)}, f32[16,128]{1,0:T(8,128)S(1)}, /*index=5*/f32[24,128]{1,0:T(8,128)S(1)}) custom-call(f32[18,36,8,128]{3,2,1,0:T(8,128)} %x.1, f32[2,4,8,128]{3,2,1,0:T(8,128)} %cur_in.1, s32[8,128]{1,0:T(8,128)} %mask_in.1, ...), custom_call_target="tpu_custom_call" | custom-call | flops 10616832 | bytes 2654208 | tf_op jit(solution)/shard_map/spectra_sums/pallas_call | solution.py:570
  3.3 3.0 %collective-permute-start = (f32[176,128]{1,0:T(8,128)S(1)}, f32[176,128]{1,0:T(8,128)S(1)}, u32[]{:S(2)}, u32[]{:S(2)}) collective-permute-start(f32[176,128]{1,0:T(8,128)S(1)} %get-tuple-element.20.mine), channel_id=1, source_target_pairs={{0,16},{16,0},{1,17},{17,1},{2,18},{18,2},{3,19},{19,3},{4,20},{20... | collective-permute-start | bytes 270344 | tf_op jit(solution)/shard_map/ppermute | solution.py:520
  6.4 0.1 collective-permute-start.3
  6.5 0.1 pick_rows.3
  6.5 3.2 %collective-permute-start.4 = (f32[324,128]{1,0:T(8,128)S(1)}, f32[324,128]{1,0:T(8,128)S(1)}, u32[]{:S(2)}, u32[]{:S(2)}) collective-permute-start(f32[324,128]{1,0:T(8,128)S(1)} %pick_rows.3), channel_id=1, source_target_pairs={{0,4},{1,5},{2,6},{3,7},{4,0},{5,1},{6,2},{7,3},{8,12},{9,13},{10,... | collective-permute-start | bytes 497672 | tf_op jit(solution)/shard_map/ppermute | solution.py:533
  9.7 0.0 collective-permute-done.other
  9.8 0.2 pack_columns.1
  9.9 0.2 collective-permute-start.1
  10.1 0.4 %collective-permute-start.2 = (f32[32,128]{1,0:T(8,128)S(1)}, f32[32,128]{1,0:T(8,128)S(1)}, u32[]{:S(2)}, u32[]{:S(2)}) collective-permute-start(f32[32,128]{1,0:T(8,128)S(1)} %get-tuple-element.26), channel_id=1, source_target_pairs={{0,1},{1,2},{2,3},{3,0},{4,5},{5,6},{6,7},{7,4},{8,9},{9,10},{10,1... | collective-permute-start | bytes 49160 | tf_op jit(solution)/shard_map/ppermute | solution.py:520
  10.5 1.1 %collective-permute-done.1.from_east = f32[32,128]{1,0:T(8,128)S(1)} collective-permute-done((f32[32,128]{1,0:T(8,128)S(1)}, f32[32,128]{1,0:T(8,128)S(1)}, u32[]{:S(2)}, u32[]{:S(2)}) %collective-permute-start.1) | collective-permute-done | bytes 16416 | tf_op jit(solution)/shard_map/ppermute | solution.py:520
  11.5 1.9 %collective-permute-done.2.from_west = f32[32,128]{1,0:T(8,128)S(1)} collective-permute-done((f32[32,128]{1,0:T(8,128)S(1)}, f32[32,128]{1,0:T(8,128)S(1)}, u32[]{:S(2)}, u32[]{:S(2)}) %collective-permute-start.2) | collective-permute-done | bytes 16416 | tf_op jit(solution)/shard_map/ppermute | solution.py:520
  13.4 0.0 collective-permute-done.3.got_rows.second
  13.4 0.2 %pack_rows.1 = (f32[4,8,128]{2,1,0:T(8,128)S(1)}, f32[32,8,128]{2,1,0:T(8,128)S(1)}, f32[112,128]{1,0:T(8,128)S(1)}, f32[112,128]{1,0:T(8,128)S(1)}) custom-call(f32[32,128]{1,0:T(8,128)S(1)} %collective-permute-done.1.from_east, f32[32,128]{1,0:T(8,128)S(1)} %collective-permute-done.2.from_west, f32[16,8,128]{2,1,0:T(8,128)S(1)} %get-tuple-element.24.fields, ...), custom_call_target="tpu_custom_call" | custom-call | flops 134217728 | bytes 262144 | tf_op jit(solution)/shard_map/pack_rows/pallas_call | solution.py:634
  13.6 1.2 %collective-permute-start.5 = (f32[112,128]{1,0:T(8,128)S(1)}, f32[112,128]{1,0:T(8,128)S(1)}, u32[]{:S(2)}, u32[]{:S(2)}) collective-permute-start(f32[112,128]{1,0:T(8,128)S(1)} %get-tuple-element.32), channel_id=1, source_target_pairs={{0,4},{1,5},{2,6},{3,7},{4,0},{5,1},{6,2},{7,3},{8,12},{9,13},{10,... | collective-permute-start | bytes 172040 | tf_op jit(solution)/shard_map/ppermute | solution.py:533
  14.8 0.0 collective-permute-start.6
  14.8 0.0 collective-permute-done.4.first
  14.8 2.5 %wave_step.1 = (f32[18,36,8,128]{3,2,1,0:T(8,128)}, f32[4,8,128]{2,1,0:T(8,128)S(1)}) custom-call(f32[18,36,8,128]{3,2,1,0:T(8,128)S(1)} %get-tuple-element.19.x, f32[16,8,128]{2,1,0:T(8,128)S(1)} %get-tuple-element.24.fields, f32[4,8,128]{2,1,0:T(8,128)S(1)} %get-tuple-element.29.coup, f32[16,128]{1,0:T(8,128)S(1)} %get-tuple-element.21.local, ...), custom_call_target="tpu_custom_call" | custom-call | flops 5971968 | bytes 5308416 | tf_op jit(solution)/shard_map/wave_step/pallas_call | solution.py:646
  17.4 0.5 %collective-permute-done.5.from_first = f32[112,128]{1,0:T(8,128)S(1)} collective-permute-done((f32[112,128]{1,0:T(8,128)S(1)}, f32[112,128]{1,0:T(8,128)S(1)}, u32[]{:S(2)}, u32[]{:S(2)}) %collective-permute-start.5) | collective-permute-done | bytes 57376 | tf_op jit(solution)/shard_map/ppermute | solution.py:533
  17.8 0.0 collective-permute-done.6.from_second
  17.8 1.1 %ocean_steps.1 = f32[2,4,8,128]{3,2,1,0:T(8,128)} custom-call(f32[112,128]{1,0:T(8,128)S(1)} %collective-permute-done.5.from_first, f32[112,128]{1,0:T(8,128)S(1)} %collective-permute-done.6.from_second, f32[16,8,128]{2,1,0:T(8,128)S(1)} %get-tuple-element.24.fields, f32[4,8,128]{2,1,0:T(8,128)S(1)} %get-tuple-element.34.coup, ...), custom_call_target="tpu_custom_call" | custom-call | flops 1048576 | bytes 1048576 | tf_op jit(solution)/shard_map/ocean_steps/pallas_call | solution.py:657
  (2 shorter events, 0.1 us)
Async XLA Ops:
  3.3 6.4 %collective-permute-start = (f32[176,128]{1,0:T(8,128)S(1)}, f32[176,128]{1,0:T(8,128)S(1)}, u32[]{:S(2)}, u32[]{:S(2)}) collective-permute-start(f32[176,128]{1,0:T(8,128)S(1)} %get-tuple-element.20.mine), channel_id=1, source_target_pairs={{0,16},{16,0},{1,17},{17,1},{2,18},{18,2},{3,19},{19,3},{4,20},{20... | collective-permute-start | bytes 270344 | tf_op jit(solution)/shard_map/ppermute | solution.py:520
  6.4 7.0 %collective-permute-start.3 = (f32[324,128]{1,0:T(8,128)S(1)}, f32[324,128]{1,0:T(8,128)S(1)}, u32[]{:S(2)}, u32[]{:S(2)}) collective-permute-start(f32[324,128]{1,0:T(8,128)S(1)} %pick_rows.2), channel_id=1, source_target_pairs={{0,1},{1,0},{2,3},{3,2},{4,8},{5,9},{6,10},{7,11},{8,4},{9,5},{10,... | collective-permute-start | bytes 497672 | tf_op jit(solution)/shard_map/ppermute | solution.py:533
  6.5 8.3 %collective-permute-start.4 = (f32[324,128]{1,0:T(8,128)S(1)}, f32[324,128]{1,0:T(8,128)S(1)}, u32[]{:S(2)}, u32[]{:S(2)}) collective-permute-start(f32[324,128]{1,0:T(8,128)S(1)} %pick_rows.3), channel_id=1, source_target_pairs={{0,4},{1,5},{2,6},{3,7},{4,0},{5,1},{6,2},{7,3},{8,12},{9,13},{10,... | collective-permute-start | bytes 497672 | tf_op jit(solution)/shard_map/ppermute | solution.py:533
  9.9 1.6 %collective-permute-start.1 = (f32[32,128]{1,0:T(8,128)S(1)}, f32[32,128]{1,0:T(8,128)S(1)}, u32[]{:S(2)}, u32[]{:S(2)}) collective-permute-start(f32[32,128]{1,0:T(8,128)S(1)} %get-tuple-element.25), channel_id=1, source_target_pairs={{0,3},{1,0},{2,1},{3,2},{4,7},{5,4},{6,5},{7,6},{8,11},{9,8},{10,9... | collective-permute-start | bytes 49160 | tf_op jit(solution)/shard_map/ppermute | solution.py:520
  10.1 3.3 %collective-permute-start.2 = (f32[32,128]{1,0:T(8,128)S(1)}, f32[32,128]{1,0:T(8,128)S(1)}, u32[]{:S(2)}, u32[]{:S(2)}) collective-permute-start(f32[32,128]{1,0:T(8,128)S(1)} %get-tuple-element.26), channel_id=1, source_target_pairs={{0,1},{1,2},{2,3},{3,0},{4,5},{5,6},{6,7},{7,4},{8,9},{9,10},{10,1... | collective-permute-start | bytes 49160 | tf_op jit(solution)/shard_map/ppermute | solution.py:520
  13.6 4.2 %collective-permute-start.5 = (f32[112,128]{1,0:T(8,128)S(1)}, f32[112,128]{1,0:T(8,128)S(1)}, u32[]{:S(2)}, u32[]{:S(2)}) collective-permute-start(f32[112,128]{1,0:T(8,128)S(1)} %get-tuple-element.32), channel_id=1, source_target_pairs={{0,4},{1,5},{2,6},{3,7},{4,0},{5,1},{6,2},{7,3},{8,12},{9,13},{10,... | collective-permute-start | bytes 172040 | tf_op jit(solution)/shard_map/ppermute | solution.py:533
  14.8 3.0 %collective-permute-start.6 = (f32[112,128]{1,0:T(8,128)S(1)}, f32[112,128]{1,0:T(8,128)S(1)}, u32[]{:S(2)}, u32[]{:S(2)}) collective-permute-start(f32[112,128]{1,0:T(8,128)S(1)} %get-tuple-element.33), channel_id=1, source_target_pairs={{0,1},{1,0},{2,3},{3,2},{4,8},{5,9},{6,10},{7,11},{8,4},{9,5},{10,... | collective-permute-start | bytes 172040 | tf_op jit(solution)/shard_map/ppermute | solution.py:533

commit v4 on v3

--- a/solution.py
+++ b/solution.py
@@ -78,7 +78,8 @@
         self.half = directions // 2
         self.per_tile = LANES // self.half
         self.col_tiles = -(-freqs // self.per_tile)
-        self.edge_rows = freqs * directions // 2
+        self.edge_rows = -(-freqs * directions // 2 // ROWS) * ROWS
+        assert self.half >= ROWS
         self.sec_sums = self.fields // 2
         self.sec_cols = self.sec_sums + SUMS
         self.sec_rows = self.sec_cols + 1
@@ -104,7 +105,7 @@
 
 def chunks(z):
     q = z.quarter
-    cuts = sorted({0, q * 4 // 9, q * 7 // 9, q})
+    cuts = sorted({0, q * 5 // 9, q})
     result = []
     for lo, hi in zip(cuts, cuts[1:]):
         starts = (lo, 2 * q - hi, 2 * q + lo, 4 * q - hi)
@@ -138,8 +139,11 @@
     for comp in range(2):
         for level in range(z.levels):
             put(pay, comp * z.levels + level, cur[comp, level] * sea)
-    for f in range(nf):
-        coef[pl.ds(f, 1), :] = jnp.full((1, LANES), courant[f], F32)
+    for t in range(z.coef_tiles):
+        tile = zero
+        for f in range(t * ROWS, min(nf, (t + 1) * ROWS)):
+            tile = jnp.where(row == f - t * ROWS, courant[f], tile)
+        put(coef, t, tile)
 
     def add(i):
         c, s = float(sizes[0, i]), float(sizes[1, i])
@@ -197,6 +201,7 @@
         put(wcol, t, west[t])
 
     cols = zero
+    rims = [zero] * (z.sec_tiles - z.sec_rows)
     for k in range(SUMS):
         center, east, west, north, south = (acc[kind * SUMS + k] for kind in range(5))
         value = center + jnp.where(lane > 0, lane_roll(east, 1), 0.0) + jnp.where(lane < LANES - 1, lane_roll(west, -1), 0.0)
@@ -204,12 +209,12 @@
         put(pay, z.sec_sums + k, value)
         cols = jnp.where(lane == k, lane_roll(east, k - (LANES - 1)), cols)
         cols = jnp.where(lane == SUMS + k, lane_roll(west, SUMS + k), cols)
-        pay[pl.ds(z.sec_rows * ROWS + k, 1), :] = north[ROWS - 1 :]
-        pay[pl.ds(z.sec_rows * ROWS + SUMS + k, 1), :] = south[:1]
+        for at, tile, edge in ((k, north, ROWS - 1), (SUMS + k, south, 0)):
+            t, r = at // ROWS, at % ROWS
+            rims[t] = jnp.where(row == r, row_roll(tile, r - edge), rims[t])
     put(pay, z.sec_cols, cols)
-    spare = (z.sec_tiles - z.sec_rows) * ROWS - 2 * SUMS
-    if spare:
-        pay[pl.ds(z.sec_tiles * ROWS - spare, spare), :] = jnp.zeros((spare, LANES), F32)
+    for t, tile in enumerate(rims):
+        put(pay, z.sec_rows + t, tile)
 
 
 def parts(tile):
@@ -221,8 +226,11 @@
     flat = x.reshape(z.freqs * z.directions * ROWS, LANES)
     north, south = ROWS - 1, z.half * ROWS
     start = jnp.where(lax.rem(lax.axis_index("lat"), 2) == turn, north, south)
+    out[pl.ds(z.edge_rows - ROWS, ROWS), :] = jnp.zeros((ROWS, LANES), F32)
     for f in range(z.freqs):
-        out[pl.ds(f * z.half, z.half), :] = flat[pl.ds(f * z.directions * ROWS + start, z.half, stride=ROWS), :]
+        for first in [*range(0, z.half - ROWS, ROWS), z.half - ROWS]:
+            eight = flat[pl.ds((f * z.directions + first) * ROWS + start, ROWS, stride=ROWS), :]
+            out[pl.ds(f * z.half + first, ROWS), :] = eight
 
 
 def picks_kernel(z, x, picks):
@@ -368,7 +376,10 @@
     sea = take(local, 0)
     zonal, meridional = current_gain * fields[top], current_gain * fields[total + top]
     coup_out[...] = coup[...]
-    sides[0], sides[1] = lat_sides(first[...], second[...], lat_count)
+    place = lax.axis_index("lat")
+    odd = lax.rem(place, 2)
+    sides[odd] = jnp.where((odd == 1) | (place < lat_count - 1), first[...], 0.0)
+    sides[1 - odd] = jnp.where((place > 0) & ((odd == 0) | (place < lat_count - 1)), second[...], 0.0)
     sizes = tables(z.directions)
     headings = []
     for i in range(q):
@@ -422,7 +433,6 @@
     total = 2 * z.levels
     row = rows()
     sec = lax.axis_index("sec")
-    top = sec * (total - 1)
     sea, diffusion = take(local, 0), take(local, 1)
     low = row < HALO
 
@@ -439,8 +449,9 @@
     halo, halo_edge = [], []
     for k in range(z.pairs):
         halo += pair(*sides(z.lat_pairs + k))
-        halo_edge += pair(lane_roll(north_edges, -2 * HALO * k), lane_roll(south_edges, -2 * HALO * k))
+        halo_edge += [lane_roll(tile, -2 * HALO * k) for tile in pair(north_edges, south_edges)]
     inner, outer, inner_edge, outer_edge = [], [], [], []
+    edge_rows = [[lane_roll(tile, -2 * HALO * (z.pairs + t)) for tile in (north_edges, south_edges)] for t in range(z.flux_tiles)]
     for k in range(SUMS):
         t, r = k // ROWS, k % ROWS
         high = row == ROWS - 1
@@ -449,9 +460,7 @@
         south = jnp.broadcast_to(south_rows[t][r : r + 1], (ROWS, LANES))
         inner.append(jnp.where(high, north, jnp.where(bottom, south, 0.0)))
         outer.append(jnp.where(bottom, spread(flux, ROWS + k), jnp.where(high, spread(flux, ROWS + SUMS + k), 0.0)))
-        shift = -2 * HALO * (z.pairs + t)
-        north = jnp.broadcast_to(lane_roll(north_edges, shift)[r : r + 1], (ROWS, LANES))
-        south = jnp.broadcast_to(lane_roll(south_edges, shift)[r : r + 1], (ROWS, LANES))
+        north, south = [jnp.broadcast_to(tile[r : r + 1], (ROWS, LANES)) for tile in edge_rows[t]]
         inner_edge.append(jnp.where(high, north, jnp.where(bottom, south, 0.0)))
         mine = edges[z.arrays + k]
         outer_edge.append(
@@ -461,12 +470,14 @@
     def joined(main, edge, halo_main, halo_side):
         return jnp.concatenate([jnp.concatenate([main, edge], axis=1), jnp.concatenate([halo_main, halo_side], axis=1)], axis=0)
 
+    whole = [joined(fields[k], edges[k], halo[k], halo_edge[k]) for k in range(z.fields)]
     for k in range(z.fields):
-        ext[k] = joined(fields[k], edges[k], halo[k], halo_edge[k])
+        ext[k] = whole[k]
+    zonal, meridional = [jnp.where(sec == 0, whole[comp * total], whole[comp * total + total - 1]) for comp in range(2)]
     sea_all = joined(sea, edges[z.fields], halo[z.fields], halo_edge[z.fields])
     kappa = joined(diffusion, edges[z.fields + 1], halo[z.fields + 1], halo_edge[z.fields + 1])
     sums = [joined(inner[k], inner_edge[k], outer[k], outer_edge[k]) for k in range(SUMS)]
-    extra = coupled(sums, ext[top], ext[total + top], sea_all)
+    extra = coupled(sums, zonal, meridional, sea_all)
     first = z.fields + 2
     coupling = [joined(coup[k], edges[first + k], halo[first + k], halo_edge[first + k]) + extra[k] for k in range(4)]
 

time: 19.1 us -> 19 us (level)
  Pallas kernels: 6.88 us -> 6.68 us
where the time goes in v4:
time: 19 us; the launch traced here: 18.8 us
  starting transfers between devices  8.02 us (42%)
  Pallas kernels  6.68 us (35%)
  waiting for transfers between devices  3.45 us (18%)
  between operations  0.69 us (4%)
    ppermute x4, starting transfers between devices, swapped(): return lax.ppermute(value, ('lat', 'lon'), pairs)  4.45 us
    ppermute x3, starting transfers between devices, shifted(): lax.ppermute(value, axis, [(i, (i + steps) % count) for i in range(count)])  3.57 us
    ppermute x3, waiting for transfers between devices, shifted(): lax.ppermute(value, axis, [(i, (i + steps) % count) for i in range(count)])  2.91 us
    pallas_call x1, Pallas kernels, shards(): call(functools.partial(sums_kernel, z), (whole, flat(z.sec_tiles), flat(z...  2.57 us
    pallas_call x1, Pallas kernels, shards(): call(functools.partial(wave_kernel, z, lat_count), (jax.ShapeDtypeStruct(...  2.47 us
    pallas_call x1, Pallas kernels, shards(): call(functools.partial(ocean_kernel, z, lat_count), (jax.ShapeDtypeStruct...  1.11 us
    ppermute x4, waiting for transfers between devices, swapped(): return lax.ppermute(value, ('lat', 'lon'), pairs)  0.54 us
  transfers between devices with their start and end apart: 7, of which 3 were waited for; matrix products, arithmetic and copies ran while one was open for 0% of the time, Pallas kernels for 16%

profile of v4, /device:TPU:0, one launch (start us, length us, event | category | flops | bytes accessed | tf_op | source)
XLA Modules:
  0.0 18.8 jit_solution(17202539641093546830)
XLA Ops:
  0.6 2.6 %spectra_sums.1 = (f32[18,36,8,128]{3,2,1,0:T(8,128)S(1)}, f32[176,128]{1,0:T(8,128)S(1)}, f32[24,128]{1,0:T(8,128)S(1)}, f32[24,128]{1,0:T(8,128)S(1)}, f32[16,128]{1,0:T(8,128)S(1)}, /*index=5*/f32[24,128]{1,0:T(8,128)S(1)}) custom-call(f32[18,36,8,128]{3,2,1,0:T(8,128)} %x.1, f32[2,4,8,128]{3,2,1,0:T(8,128)} %cur_in.1, s32[8,128]{1,0:T(8,128)} %mask_in.1, ...), custom_call_target="tpu_custom_call" | custom-call | flops 10616832 | bytes 2654208 | tf_op jit(solution)/shard_map/spectra_sums/pallas_call | solution.py:581
  3.2 3.0 %collective-permute-start = (f32[176,128]{1,0:T(8,128)S(1)}, f32[176,128]{1,0:T(8,128)S(1)}, u32[]{:S(2)}, u32[]{:S(2)}) collective-permute-start(f32[176,128]{1,0:T(8,128)S(1)} %get-tuple-element.20.mine), channel_id=1, source_target_pairs={{0,16},{16,0},{1,17},{17,1},{2,18},{18,2},{3,19},{19,3},{4,20},{20... | collective-permute-start | bytes 270344 | tf_op jit(solution)/shard_map/ppermute | solution.py:531
  6.2 0.1 pick_rows.2
  6.3 0.1 collective-permute-start.3
  6.4 0.1 pick_rows.3
  6.4 3.2 %collective-permute-start.4 = (f32[328,128]{1,0:T(8,128)S(1)}, f32[328,128]{1,0:T(8,128)S(1)}, u32[]{:S(2)}, u32[]{:S(2)}) collective-permute-start(f32[328,128]{1,0:T(8,128)S(1)} %pick_rows.3), channel_id=1, source_target_pairs={{0,4},{1,5},{2,6},{3,7},{4,0},{5,1},{6,2},{7,3},{8,12},{9,13},{10,... | collective-permute-start | bytes 503816 | tf_op jit(solution)/shard_map/ppermute | solution.py:544
  9.6 0.0 collective-permute-done.other
  9.7 0.2 pack_columns.1
  9.8 0.2 collective-permute-start.1
  10.0 0.4 %collective-permute-start.2 = (f32[32,128]{1,0:T(8,128)S(1)}, f32[32,128]{1,0:T(8,128)S(1)}, u32[]{:S(2)}, u32[]{:S(2)}) collective-permute-start(f32[32,128]{1,0:T(8,128)S(1)} %get-tuple-element.26), channel_id=1, source_target_pairs={{0,1},{1,2},{2,3},{3,0},{4,5},{5,6},{6,7},{7,4},{8,9},{9,10},{10,1... | collective-permute-start | bytes 49160 | tf_op jit(solution)/shard_map/ppermute | solution.py:531
  10.4 1.1 %collective-permute-done.1.from_east = f32[32,128]{1,0:T(8,128)S(1)} collective-permute-done((f32[32,128]{1,0:T(8,128)S(1)}, f32[32,128]{1,0:T(8,128)S(1)}, u32[]{:S(2)}, u32[]{:S(2)}) %collective-permute-start.1) | collective-permute-done | bytes 16416 | tf_op jit(solution)/shard_map/ppermute | solution.py:531
  11.4 1.9 %collective-permute-done.2.from_west = f32[32,128]{1,0:T(8,128)S(1)} collective-permute-done((f32[32,128]{1,0:T(8,128)S(1)}, f32[32,128]{1,0:T(8,128)S(1)}, u32[]{:S(2)}, u32[]{:S(2)}) %collective-permute-start.2) | collective-permute-done | bytes 16416 | tf_op jit(solution)/shard_map/ppermute | solution.py:531
  13.3 0.0 collective-permute-done.3.got_rows.second
  13.3 0.2 %pack_rows.1 = (f32[4,8,128]{2,1,0:T(8,128)S(1)}, f32[32,8,128]{2,1,0:T(8,128)S(1)}, f32[112,128]{1,0:T(8,128)S(1)}, f32[112,128]{1,0:T(8,128)S(1)}) custom-call(f32[32,128]{1,0:T(8,128)S(1)} %collective-permute-done.1.from_east, f32[32,128]{1,0:T(8,128)S(1)} %collective-permute-done.2.from_west, f32[16,8,128]{2,1,0:T(8,128)S(1)} %get-tuple-element.24.fields, ...), custom_call_target="tpu_custom_call" | custom-call | flops 134217728 | bytes 262144 | tf_op jit(solution)/shard_map/pack_rows/pallas_call | solution.py:645
  13.5 1.2 %collective-permute-start.5 = (f32[112,128]{1,0:T(8,128)S(1)}, f32[112,128]{1,0:T(8,128)S(1)}, u32[]{:S(2)}, u32[]{:S(2)}) collective-permute-start(f32[112,128]{1,0:T(8,128)S(1)} %get-tuple-element.32), channel_id=1, source_target_pairs={{0,4},{1,5},{2,6},{3,7},{4,0},{5,1},{6,2},{7,3},{8,12},{9,13},{10,... | collective-permute-start | bytes 172040 | tf_op jit(solution)/shard_map/ppermute | solution.py:544
  14.7 0.0 collective-permute-start.6
  14.7 0.0 collective-permute-done.4.first
  14.7 2.5 %wave_step.1 = (f32[18,36,8,128]{3,2,1,0:T(8,128)}, f32[4,8,128]{2,1,0:T(8,128)S(1)}) custom-call(f32[18,36,8,128]{3,2,1,0:T(8,128)S(1)} %get-tuple-element.19.x, f32[16,8,128]{2,1,0:T(8,128)S(1)} %get-tuple-element.24.fields, f32[4,8,128]{2,1,0:T(8,128)S(1)} %get-tuple-element.29.coup, f32[16,128]{1,0:T(8,128)S(1)} %get-tuple-element.21.local, ...), custom_call_target="tpu_custom_call" | custom-call | flops 5971968 | bytes 5308416 | tf_op jit(solution)/shard_map/wave_step/pallas_call | solution.py:657
  17.2 0.5 %collective-permute-done.5.from_first = f32[112,128]{1,0:T(8,128)S(1)} collective-permute-done((f32[112,128]{1,0:T(8,128)S(1)}, f32[112,128]{1,0:T(8,128)S(1)}, u32[]{:S(2)}, u32[]{:S(2)}) %collective-permute-start.5) | collective-permute-done | bytes 57376 | tf_op jit(solution)/shard_map/ppermute | solution.py:544
  17.7 0.0 collective-permute-done.6.from_second
  17.7 1.1 %ocean_steps.1 = f32[2,4,8,128]{3,2,1,0:T(8,128)} custom-call(f32[112,128]{1,0:T(8,128)S(1)} %collective-permute-done.5.from_first, f32[112,128]{1,0:T(8,128)S(1)} %collective-permute-done.6.from_second, f32[16,8,128]{2,1,0:T(8,128)S(1)} %get-tuple-element.24.fields, f32[4,8,128]{2,1,0:T(8,128)S(1)} %get-tuple-element.34.coup, ...), custom_call_target="tpu_custom_call" | custom-call | flops 1048576 | bytes 1048576 | tf_op jit(solution)/shard_map/ocean_steps/pallas_call | solution.py:668
  (1 shorter events, 0.0 us)
Async XLA Ops:
  3.2 6.4 %collective-permute-start = (f32[176,128]{1,0:T(8,128)S(1)}, f32[176,128]{1,0:T(8,128)S(1)}, u32[]{:S(2)}, u32[]{:S(2)}) collective-permute-start(f32[176,128]{1,0:T(8,128)S(1)} %get-tuple-element.20.mine), channel_id=1, source_target_pairs={{0,16},{16,0},{1,17},{17,1},{2,18},{18,2},{3,19},{19,3},{4,20},{20... | collective-permute-start | bytes 270344 | tf_op jit(solution)/shard_map/ppermute | solution.py:531
  6.3 7.0 %collective-permute-start.3 = (f32[328,128]{1,0:T(8,128)S(1)}, f32[328,128]{1,0:T(8,128)S(1)}, u32[]{:S(2)}, u32[]{:S(2)}) collective-permute-start(f32[328,128]{1,0:T(8,128)S(1)} %pick_rows.2), channel_id=1, source_target_pairs={{0,1},{1,0},{2,3},{3,2},{4,8},{5,9},{6,10},{7,11},{8,4},{9,5},{10,... | collective-permute-start | bytes 503816 | tf_op jit(solution)/shard_map/ppermute | solution.py:544
  6.4 8.3 %collective-permute-start.4 = (f32[328,128]{1,0:T(8,128)S(1)}, f32[328,128]{1,0:T(8,128)S(1)}, u32[]{:S(2)}, u32[]{:S(2)}) collective-permute-start(f32[328,128]{1,0:T(8,128)S(1)} %pick_rows.3), channel_id=1, source_target_pairs={{0,4},{1,5},{2,6},{3,7},{4,0},{5,1},{6,2},{7,3},{8,12},{9,13},{10,... | collective-permute-start | bytes 503816 | tf_op jit(solution)/shard_map/ppermute | solution.py:544
  9.8 1.6 %collective-permute-start.1 = (f32[32,128]{1,0:T(8,128)S(1)}, f32[32,128]{1,0:T(8,128)S(1)}, u32[]{:S(2)}, u32[]{:S(2)}) collective-permute-start(f32[32,128]{1,0:T(8,128)S(1)} %get-tuple-element.25), channel_id=1, source_target_pairs={{0,3},{1,0},{2,1},{3,2},{4,7},{5,4},{6,5},{7,6},{8,11},{9,8},{10,9... | collective-permute-start | bytes 49160 | tf_op jit(solution)/shard_map/ppermute | solution.py:531
  10.0 3.3 %collective-permute-start.2 = (f32[32,128]{1,0:T(8,128)S(1)}, f32[32,128]{1,0:T(8,128)S(1)}, u32[]{:S(2)}, u32[]{:S(2)}) collective-permute-start(f32[32,128]{1,0:T(8,128)S(1)} %get-tuple-element.26), channel_id=1, source_target_pairs={{0,1},{1,2},{2,3},{3,0},{4,5},{5,6},{6,7},{7,4},{8,9},{9,10},{10,1... | collective-permute-start | bytes 49160 | tf_op jit(solution)/shard_map/ppermute | solution.py:531
  13.5 4.2 %collective-permute-start.5 = (f32[112,128]{1,0:T(8,128)S(1)}, f32[112,128]{1,0:T(8,128)S(1)}, u32[]{:S(2)}, u32[]{:S(2)}) collective-permute-start(f32[112,128]{1,0:T(8,128)S(1)} %get-tuple-element.32), channel_id=1, source_target_pairs={{0,4},{1,5},{2,6},{3,7},{4,0},{5,1},{6,2},{7,3},{8,12},{9,13},{10,... | collective-permute-start | bytes 172040 | tf_op jit(solution)/shard_map/ppermute | solution.py:544
  14.7 3.0 %collective-permute-start.6 = (f32[112,128]{1,0:T(8,128)S(1)}, f32[112,128]{1,0:T(8,128)S(1)}, u32[]{:S(2)}, u32[]{:S(2)}) collective-permute-start(f32[112,128]{1,0:T(8,128)S(1)} %get-tuple-element.33), channel_id=1, source_target_pairs={{0,1},{1,0},{2,3},{3,2},{4,8},{5,9},{6,10},{7,11},{8,4},{9,5},{10,... | collective-permute-start | bytes 172040 | tf_op jit(solution)/shard_map/ppermute | solution.py:544

commit v5 on v4

--- a/solution.py
+++ b/solution.py
@@ -88,15 +88,20 @@
         self.lon_flux = self.lon_coup + 4 * HALO
         self.lon_rows = self.lon_flux + SUMS
         self.arrays = self.fields + 2 + 4
-        self.pairs = self.arrays // 2
+        total = 2 * levels
+        assert ITERS <= HALO and HALO + levels - 1 - (total - 2) <= 2
+        self.short = [comp * total + p for comp in range(2) for p in range(total - 2, total)]
+        self.long = [k for k in range(self.arrays) if k not in self.short]
+        self.pairs = len(self.long) // 2
+        self.bodies = self.pairs + 1
         self.flux_tiles = -(-SUMS // ROWS)
         self.lat_pairs = 0
-        self.lat_flux = self.lat_pairs + self.pairs
+        self.lat_flux = self.lat_pairs + self.bodies
         self.lat_edges = self.lat_flux + self.flux_tiles
         self.lat_tiles = self.lat_edges + 1
         self.coef_tiles = -(-freqs // ROWS)
         assert self.lon_rows + SUMS * FLUX_COLS <= LANES
-        assert (self.pairs + self.flux_tiles) * 2 * HALO <= LANES
+        assert (self.bodies + self.flux_tiles) * 2 * HALO <= LANES
 
     def headings(self, i):
         q = self.quarter
@@ -331,10 +336,22 @@
 
     north_edges = jnp.zeros((ROWS, LANES), F32)
     south_edges = north_edges
-    for k in range(z.pairs):
-        north, south = pair(main[2 * k], main[2 * k + 1])
-        send(z.lat_pairs + k, north, south)
-        north, south = pair(edge[2 * k], edge[2 * k + 1])
+    def four(tiles):
+        north, south = tiles[0], tiles[0]
+        for j in range(1, 4):
+            north = jnp.where(lax.div(row, 2) == 3 - j, row_roll(tiles[j], -2 * j), north)
+            south = jnp.where(lax.div(row, 2) == j, row_roll(tiles[j], 2 * j), south)
+        return north, south
+
+    for k in range(z.bodies):
+        both = []
+        for arrays in (main, edge):
+            if k < z.pairs:
+                both.append(pair(*[arrays[n] for n in z.long[2 * k : 2 * k + 2]]))
+            else:
+                both.append(four([arrays[n] for n in z.short]))
+        send(z.lat_pairs + k, *both[0])
+        north, south = both[1]
         in_group, moved = group(north, k)
         north_edges = jnp.where(in_group, moved, north_edges)
         in_group, moved = group(south, k)
@@ -349,9 +366,9 @@
             north_row = jnp.where(row == r, jnp.broadcast_to(row_edge[k][ROWS - 1 :], (ROWS, LANES)), north_row)
             south_row = jnp.where(row == r, jnp.broadcast_to(row_edge[k][:1], (ROWS, LANES)), south_row)
         send(z.lat_flux + t, north, south)
-        in_group, moved = group(north_row, z.pairs + t)
+        in_group, moved = group(north_row, z.bodies + t)
         north_edges = jnp.where(in_group, moved, north_edges)
-        in_group, moved = group(south_row, z.pairs + t)
+        in_group, moved = group(south_row, z.bodies + t)
         south_edges = jnp.where(in_group, moved, south_edges)
     send(z.lat_edges, north_edges, south_edges)
 
@@ -446,12 +463,16 @@
 
     north_edges, south_edges = sides(z.lat_edges)
     north_rows, south_rows = zip(*[sides(z.lat_flux + t) for t in range(z.flux_tiles)])
-    halo, halo_edge = [], []
-    for k in range(z.pairs):
-        halo += pair(*sides(z.lat_pairs + k))
-        halo_edge += [lane_roll(tile, -2 * HALO * k) for tile in pair(north_edges, south_edges)]
+    def four(north, south):
+        return [jnp.where(row < 2, row_roll(north, -2 * j), jnp.where(row >= ROWS - 2, row_roll(south, 2 * j), 0.0)) for j in range(4)]
+
+    halo, halo_edge = {}, {}
+    for k in range(z.bodies):
+        places, split = (z.long[2 * k : 2 * k + 2], pair) if k < z.pairs else (z.short, four)
+        halo.update(zip(places, split(*sides(z.lat_pairs + k))))
+        halo_edge.update(zip(places, [lane_roll(tile, -2 * HALO * k) for tile in split(north_edges, south_edges)]))
     inner, outer, inner_edge, outer_edge = [], [], [], []
-    edge_rows = [[lane_roll(tile, -2 * HALO * (z.pairs + t)) for tile in (north_edges, south_edges)] for t in range(z.flux_tiles)]
+    edge_rows = [[lane_roll(tile, -2 * HALO * (z.bodies + t)) for tile in (north_edges, south_edges)] for t in range(z.flux_tiles)]
     for k in range(SUMS):
         t, r = k // ROWS, k % ROWS
         high = row == ROWS - 1

time: 19 us -> 19 us (level)
  no operation moved by 1% of the time
where the time goes in v5:
time: 19 us; the launch traced here: 18.8 us
  starting transfers between devices  8.02 us (42%)
  Pallas kernels  6.69 us (35%)
  waiting for transfers between devices  3.4 us (18%)
  between operations  0.69 us (4%)
    ppermute x4, starting transfers between devices, swapped(): return lax.ppermute(value, ('lat', 'lon'), pairs)  4.45 us
    ppermute x3, starting transfers between devices, shifted(): lax.ppermute(value, axis, [(i, (i + steps) % count) for i in range(count)])  3.57 us
    ppermute x3, waiting for transfers between devices, shifted(): lax.ppermute(value, axis, [(i, (i + steps) % count) for i in range(count)])  2.91 us
    pallas_call x1, Pallas kernels, shards(): call(functools.partial(sums_kernel, z), (whole, flat(z.sec_tiles), flat(z...  2.57 us
    pallas_call x1, Pallas kernels, shards(): call(functools.partial(wave_kernel, z, lat_count), (jax.ShapeDtypeStruct(...  2.47 us
    pallas_call x1, Pallas kernels, shards(): call(functools.partial(ocean_kernel, z, lat_count), (jax.ShapeDtypeStruct...  1.11 us
    ppermute x4, waiting for transfers between devices, swapped(): return lax.ppermute(value, ('lat', 'lon'), pairs)  0.5 us
  transfers between devices with their start and end apart: 7, of which 3 were waited for; matrix products, arithmetic and copies ran while one was open for 0% of the time, Pallas kernels for 16%

profile of v5, /device:TPU:0, one launch (start us, length us, event | category | flops | bytes accessed | tf_op | source)
XLA Modules:
  0.0 18.8 jit_solution(5232327484298373567)
XLA Ops:
  0.6 2.6 %spectra_sums.1 = (f32[18,36,8,128]{3,2,1,0:T(8,128)S(1)}, f32[176,128]{1,0:T(8,128)S(1)}, f32[24,128]{1,0:T(8,128)S(1)}, f32[24,128]{1,0:T(8,128)S(1)}, f32[16,128]{1,0:T(8,128)S(1)}, /*index=5*/f32[24,128]{1,0:T(8,128)S(1)}) custom-call(f32[18,36,8,128]{3,2,1,0:T(8,128)} %x.1, f32[2,4,8,128]{3,2,1,0:T(8,128)} %cur_in.1, s32[8,128]{1,0:T(8,128)} %mask_in.1, ...), custom_call_target="tpu_custom_call" | custom-call | flops 10616832 | bytes 2654208 | tf_op jit(solution)/shard_map/spectra_sums/pallas_call | solution.py:602
  3.2 3.0 %collective-permute-start = (f32[176,128]{1,0:T(8,128)S(1)}, f32[176,128]{1,0:T(8,128)S(1)}, u32[]{:S(2)}, u32[]{:S(2)}) collective-permute-start(f32[176,128]{1,0:T(8,128)S(1)} %get-tuple-element.20.mine), channel_id=1, source_target_pairs={{0,16},{16,0},{1,17},{17,1},{2,18},{18,2},{3,19},{19,3},{4,20},{20... | collective-permute-start | bytes 270344 | tf_op jit(solution)/shard_map/ppermute | solution.py:552
  6.2 0.1 pick_rows.2
  6.3 0.1 collective-permute-start.3
  6.4 0.1 pick_rows.3
  6.4 3.2 %collective-permute-start.4 = (f32[328,128]{1,0:T(8,128)S(1)}, f32[328,128]{1,0:T(8,128)S(1)}, u32[]{:S(2)}, u32[]{:S(2)}) collective-permute-start(f32[328,128]{1,0:T(8,128)S(1)} %pick_rows.3), channel_id=1, source_target_pairs={{0,4},{1,5},{2,6},{3,7},{4,0},{5,1},{6,2},{7,3},{8,12},{9,13},{10,... | collective-permute-start | bytes 503816 | tf_op jit(solution)/shard_map/ppermute | solution.py:565
  9.6 0.0 collective-permute-done.other
  9.7 0.2 pack_columns.1
  9.8 0.2 collective-permute-start.1
  10.0 0.4 %collective-permute-start.2 = (f32[32,128]{1,0:T(8,128)S(1)}, f32[32,128]{1,0:T(8,128)S(1)}, u32[]{:S(2)}, u32[]{:S(2)}) collective-permute-start(f32[32,128]{1,0:T(8,128)S(1)} %get-tuple-element.26), channel_id=1, source_target_pairs={{0,1},{1,2},{2,3},{3,0},{4,5},{5,6},{6,7},{7,4},{8,9},{9,10},{10,1... | collective-permute-start | bytes 49160 | tf_op jit(solution)/shard_map/ppermute | solution.py:552
  10.4 1.1 %collective-permute-done.1.from_east = f32[32,128]{1,0:T(8,128)S(1)} collective-permute-done((f32[32,128]{1,0:T(8,128)S(1)}, f32[32,128]{1,0:T(8,128)S(1)}, u32[]{:S(2)}, u32[]{:S(2)}) %collective-permute-start.1) | collective-permute-done | bytes 16416 | tf_op jit(solution)/shard_map/ppermute | solution.py:552
  11.4 1.9 %collective-permute-done.2.from_west = f32[32,128]{1,0:T(8,128)S(1)} collective-permute-done((f32[32,128]{1,0:T(8,128)S(1)}, f32[32,128]{1,0:T(8,128)S(1)}, u32[]{:S(2)}, u32[]{:S(2)}) %collective-permute-start.2) | collective-permute-done | bytes 16416 | tf_op jit(solution)/shard_map/ppermute | solution.py:552
  13.3 0.0 collective-permute-done.3.got_rows.second
  13.3 0.2 %pack_rows.1 = (f32[4,8,128]{2,1,0:T(8,128)S(1)}, f32[32,8,128]{2,1,0:T(8,128)S(1)}, f32[104,128]{1,0:T(8,128)S(1)}, f32[104,128]{1,0:T(8,128)S(1)}) custom-call(f32[32,128]{1,0:T(8,128)S(1)} %collective-permute-done.1.from_east, f32[32,128]{1,0:T(8,128)S(1)} %collective-permute-done.2.from_west, f32[16,8,128]{2,1,0:T(8,128)S(1)} %get-tuple-element.24.fields, ...), custom_call_target="tpu_custom_call" | custom-call | flops 134217728 | bytes 262144 | tf_op jit(solution)/shard_map/pack_rows/pallas_call | solution.py:666
  13.5 1.2 %collective-permute-start.5 = (f32[104,128]{1,0:T(8,128)S(1)}, f32[104,128]{1,0:T(8,128)S(1)}, u32[]{:S(2)}, u32[]{:S(2)}) collective-permute-start(f32[104,128]{1,0:T(8,128)S(1)} %get-tuple-element.32), channel_id=1, source_target_pairs={{0,4},{1,5},{2,6},{3,7},{4,0},{5,1},{6,2},{7,3},{8,12},{9,13},{10,... | collective-permute-start | bytes 159752 | tf_op jit(solution)/shard_map/ppermute | solution.py:565
  14.7 0.0 collective-permute-start.6
  14.7 0.0 collective-permute-done.4.first
  14.7 2.5 %wave_step.1 = (f32[18,36,8,128]{3,2,1,0:T(8,128)}, f32[4,8,128]{2,1,0:T(8,128)S(1)}) custom-call(f32[18,36,8,128]{3,2,1,0:T(8,128)S(1)} %get-tuple-element.19.x, f32[16,8,128]{2,1,0:T(8,128)S(1)} %get-tuple-element.24.fields, f32[4,8,128]{2,1,0:T(8,128)S(1)} %get-tuple-element.29.coup, f32[16,128]{1,0:T(8,128)S(1)} %get-tuple-element.21.local, ...), custom_call_target="tpu_custom_call" | custom-call | flops 5971968 | bytes 5308416 | tf_op jit(solution)/shard_map/wave_step/pallas_call | solution.py:678
  17.2 0.5 %collective-permute-done.5.from_first = f32[104,128]{1,0:T(8,128)S(1)} collective-permute-done((f32[104,128]{1,0:T(8,128)S(1)}, f32[104,128]{1,0:T(8,128)S(1)}, u32[]{:S(2)}, u32[]{:S(2)}) %collective-permute-start.5) | collective-permute-done | bytes 53280 | tf_op jit(solution)/shard_map/ppermute | solution.py:565
  17.7 0.0 collective-permute-done.6.from_second
  17.7 1.1 %ocean_steps.1 = f32[2,4,8,128]{3,2,1,0:T(8,128)} custom-call(f32[104,128]{1,0:T(8,128)S(1)} %collective-permute-done.5.from_first, f32[104,128]{1,0:T(8,128)S(1)} %collective-permute-done.6.from_second, f32[16,8,128]{2,1,0:T(8,128)S(1)} %get-tuple-element.24.fields, f32[4,8,128]{2,1,0:T(8,128)S(1)} %get-tuple-element.34.coup, ...), custom_call_target="tpu_custom_call" | custom-call | flops 1048576 | bytes 1048576 | tf_op jit(solution)/shard_map/ocean_steps/pallas_call | solution.py:689
  (1 shorter events, 0.0 us)
Async XLA Ops:
  3.2 6.4 %collective-permute-start = (f32[176,128]{1,0:T(8,128)S(1)}, f32[176,128]{1,0:T(8,128)S(1)}, u32[]{:S(2)}, u32[]{:S(2)}) collective-permute-start(f32[176,128]{1,0:T(8,128)S(1)} %get-tuple-element.20.mine), channel_id=1, source_target_pairs={{0,16},{16,0},{1,17},{17,1},{2,18},{18,2},{3,19},{19,3},{4,20},{20... | collective-permute-start | bytes 270344 | tf_op jit(solution)/shard_map/ppermute | solution.py:552
  6.3 7.0 %collective-permute-start.3 = (f32[328,128]{1,0:T(8,128)S(1)}, f32[328,128]{1,0:T(8,128)S(1)}, u32[]{:S(2)}, u32[]{:S(2)}) collective-permute-start(f32[328,128]{1,0:T(8,128)S(1)} %pick_rows.2), channel_id=1, source_target_pairs={{0,1},{1,0},{2,3},{3,2},{4,8},{5,9},{6,10},{7,11},{8,4},{9,5},{10,... | collective-permute-start | bytes 503816 | tf_op jit(solution)/shard_map/ppermute | solution.py:565
  6.4 8.3 %collective-permute-start.4 = (f32[328,128]{1,0:T(8,128)S(1)}, f32[328,128]{1,0:T(8,128)S(1)}, u32[]{:S(2)}, u32[]{:S(2)}) collective-permute-start(f32[328,128]{1,0:T(8,128)S(1)} %pick_rows.3), channel_id=1, source_target_pairs={{0,4},{1,5},{2,6},{3,7},{4,0},{5,1},{6,2},{7,3},{8,12},{9,13},{10,... | collective-permute-start | bytes 503816 | tf_op jit(solution)/shard_map/ppermute | solution.py:565
  9.8 1.6 %collective-permute-start.1 = (f32[32,128]{1,0:T(8,128)S(1)}, f32[32,128]{1,0:T(8,128)S(1)}, u32[]{:S(2)}, u32[]{:S(2)}) collective-permute-start(f32[32,128]{1,0:T(8,128)S(1)} %get-tuple-element.25), channel_id=1, source_target_pairs={{0,3},{1,0},{2,1},{3,2},{4,7},{5,4},{6,5},{7,6},{8,11},{9,8},{10,9... | collective-permute-start | bytes 49160 | tf_op jit(solution)/shard_map/ppermute | solution.py:552
  10.0 3.3 %collective-permute-start.2 = (f32[32,128]{1,0:T(8,128)S(1)}, f32[32,128]{1,0:T(8,128)S(1)}, u32[]{:S(2)}, u32[]{:S(2)}) collective-permute-start(f32[32,128]{1,0:T(8,128)S(1)} %get-tuple-element.26), channel_id=1, source_target_pairs={{0,1},{1,2},{2,3},{3,0},{4,5},{5,6},{6,7},{7,4},{8,9},{9,10},{10,1... | collective-permute-start | bytes 49160 | tf_op jit(solution)/shard_map/ppermute | solution.py:552
  13.5 4.2 %collective-permute-start.5 = (f32[104,128]{1,0:T(8,128)S(1)}, f32[104,128]{1,0:T(8,128)S(1)}, u32[]{:S(2)}, u32[]{:S(2)}) collective-permute-start(f32[104,128]{1,0:T(8,128)S(1)} %get-tuple-element.32), channel_id=1, source_target_pairs={{0,4},{1,5},{2,6},{3,7},{4,0},{5,1},{6,2},{7,3},{8,12},{9,13},{10,... | collective-permute-start | bytes 159752 | tf_op jit(solution)/shard_map/ppermute | solution.py:565
  14.7 3.0 %collective-permute-start.6 = (f32[104,128]{1,0:T(8,128)S(1)}, f32[104,128]{1,0:T(8,128)S(1)}, u32[]{:S(2)}, u32[]{:S(2)}) collective-permute-start(f32[104,128]{1,0:T(8,128)S(1)} %get-tuple-element.33), channel_id=1, source_target_pairs={{0,1},{1,0},{2,3},{3,2},{4,8},{5,9},{6,10},{7,11},{8,4},{9,5},{10,... | collective-permute-start | bytes 159752 | tf_op jit(solution)/shard_map/ppermute | solution.py:565

commit v6 on v4

--- a/solution.py
+++ b/solution.py
@@ -117,13 +117,11 @@
     q, nf = z.quarter, z.freqs
     pairs = ((cur_in, cur), (mask_in, mask), (diffusion_in, local.at[pl.ds(ROWS, ROWS)]), (courant_in, courant), (stokes_in, stokes), (stress_in, stress))
     small = [pltpu.make_async_copy(source, target, small_sems.at[k]) for k, (source, target) in enumerate(pairs)]
-    for copy in small:
-        copy.start()
     copies = []
     for g, (_, _, spans) in enumerate(chunks(z)):
         for j, span in enumerate(spans):
             copies.append(pltpu.make_async_copy(x.at[:, span], buf.at[:, span], sems.at[4 * g + j]))
-    for copy in copies:
+    for copy in copies + small:
         copy.start()
 
     lane, row = lanes(), rows()

time: 19 us -> 19 us (level)
  no operation moved by 1% of the time
where the time goes in v6:
time: 19 us; the launch traced here: 18.8 us
  starting transfers between devices  8.02 us (42%)
  Pallas kernels  6.67 us (35%)
  waiting for transfers between devices  3.45 us (18%)
  between operations  0.69 us (4%)
    ppermute x4, starting transfers between devices, swapped(): return lax.ppermute(value, ('lat', 'lon'), pairs)  4.45 us
    ppermute x3, starting transfers between devices, shifted(): lax.ppermute(value, axis, [(i, (i + steps) % count) for i in range(count)])  3.57 us
    ppermute x3, waiting for transfers between devices, shifted(): lax.ppermute(value, axis, [(i, (i + steps) % count) for i in range(count)])  2.91 us
    pallas_call x1, Pallas kernels, shards(): call(functools.partial(sums_kernel, z), (whole, flat(z.sec_tiles), flat(z...  2.56 us
    pallas_call x1, Pallas kernels, shards(): call(functools.partial(wave_kernel, z, lat_count), (jax.ShapeDtypeStruct(...  2.47 us
    pallas_call x1, Pallas kernels, shards(): call(functools.partial(ocean_kernel, z, lat_count), (jax.ShapeDtypeStruct...  1.11 us
    ppermute x4, waiting for transfers between devices, swapped(): return lax.ppermute(value, ('lat', 'lon'), pairs)  0.54 us
  transfers between devices with their start and end apart: 7, of which 3 were waited for; matrix products, arithmetic and copies ran while one was open for 0% of the time, Pallas kernels for 16%

profile of v6, /device:TPU:0, one launch (start us, length us, event | category | flops | bytes accessed | tf_op | source)
XLA Modules:
  0.0 18.8 jit_solution(8621634958681414688)
XLA Ops:
  0.6 2.6 %spectra_sums.1 = (f32[18,36,8,128]{3,2,1,0:T(8,128)S(1)}, f32[176,128]{1,0:T(8,128)S(1)}, f32[24,128]{1,0:T(8,128)S(1)}, f32[24,128]{1,0:T(8,128)S(1)}, f32[16,128]{1,0:T(8,128)S(1)}, /*index=5*/f32[24,128]{1,0:T(8,128)S(1)}) custom-call(f32[18,36,8,128]{3,2,1,0:T(8,128)} %x.1, f32[2,4,8,128]{3,2,1,0:T(8,128)} %cur_in.1, s32[8,128]{1,0:T(8,128)} %mask_in.1, ...), custom_call_target="tpu_custom_call" | custom-call | flops 10616832 | bytes 2654208 | tf_op jit(solution)/shard_map/spectra_sums/pallas_call | solution.py:579
  3.2 3.0 %collective-permute-start = (f32[176,128]{1,0:T(8,128)S(1)}, f32[176,128]{1,0:T(8,128)S(1)}, u32[]{:S(2)}, u32[]{:S(2)}) collective-permute-start(f32[176,128]{1,0:T(8,128)S(1)} %get-tuple-element.20.mine), channel_id=1, source_target_pairs={{0,16},{16,0},{1,17},{17,1},{2,18},{18,2},{3,19},{19,3},{4,20},{20... | collective-permute-start | bytes 270344 | tf_op jit(solution)/shard_map/ppermute | solution.py:529
  6.2 0.1 pick_rows.2
  6.3 0.1 collective-permute-start.3
  6.3 0.1 pick_rows.3
  6.4 3.2 %collective-permute-start.4 = (f32[328,128]{1,0:T(8,128)S(1)}, f32[328,128]{1,0:T(8,128)S(1)}, u32[]{:S(2)}, u32[]{:S(2)}) collective-permute-start(f32[328,128]{1,0:T(8,128)S(1)} %pick_rows.3), channel_id=1, source_target_pairs={{0,4},{1,5},{2,6},{3,7},{4,0},{5,1},{6,2},{7,3},{8,12},{9,13},{10,... | collective-permute-start | bytes 503816 | tf_op jit(solution)/shard_map/ppermute | solution.py:542
  9.6 0.0 collective-permute-done.other
  9.6 0.2 pack_columns.1
  9.8 0.2 collective-permute-start.1
  10.0 0.4 %collective-permute-start.2 = (f32[32,128]{1,0:T(8,128)S(1)}, f32[32,128]{1,0:T(8,128)S(1)}, u32[]{:S(2)}, u32[]{:S(2)}) collective-permute-start(f32[32,128]{1,0:T(8,128)S(1)} %get-tuple-element.26), channel_id=1, source_target_pairs={{0,1},{1,2},{2,3},{3,0},{4,5},{5,6},{6,7},{7,4},{8,9},{9,10},{10,1... | collective-permute-start | bytes 49160 | tf_op jit(solution)/shard_map/ppermute | solution.py:529
  10.4 1.1 %collective-permute-done.1.from_east = f32[32,128]{1,0:T(8,128)S(1)} collective-permute-done((f32[32,128]{1,0:T(8,128)S(1)}, f32[32,128]{1,0:T(8,128)S(1)}, u32[]{:S(2)}, u32[]{:S(2)}) %collective-permute-start.1) | collective-permute-done | bytes 16416 | tf_op jit(solution)/shard_map/ppermute | solution.py:529
  11.4 1.9 %collective-permute-done.2.from_west = f32[32,128]{1,0:T(8,128)S(1)} collective-permute-done((f32[32,128]{1,0:T(8,128)S(1)}, f32[32,128]{1,0:T(8,128)S(1)}, u32[]{:S(2)}, u32[]{:S(2)}) %collective-permute-start.2) | collective-permute-done | bytes 16416 | tf_op jit(solution)/shard_map/ppermute | solution.py:529
  13.3 0.0 collective-permute-done.3.got_rows.second
  13.3 0.2 %pack_rows.1 = (f32[4,8,128]{2,1,0:T(8,128)S(1)}, f32[32,8,128]{2,1,0:T(8,128)S(1)}, f32[112,128]{1,0:T(8,128)S(1)}, f32[112,128]{1,0:T(8,128)S(1)}) custom-call(f32[32,128]{1,0:T(8,128)S(1)} %collective-permute-done.1.from_east, f32[32,128]{1,0:T(8,128)S(1)} %collective-permute-done.2.from_west, f32[16,8,128]{2,1,0:T(8,128)S(1)} %get-tuple-element.24.fields, ...), custom_call_target="tpu_custom_call" | custom-call | flops 134217728 | bytes 262144 | tf_op jit(solution)/shard_map/pack_rows/pallas_call | solution.py:643
  13.5 1.2 %collective-permute-start.5 = (f32[112,128]{1,0:T(8,128)S(1)}, f32[112,128]{1,0:T(8,128)S(1)}, u32[]{:S(2)}, u32[]{:S(2)}) collective-permute-start(f32[112,128]{1,0:T(8,128)S(1)} %get-tuple-element.32), channel_id=1, source_target_pairs={{0,4},{1,5},{2,6},{3,7},{4,0},{5,1},{6,2},{7,3},{8,12},{9,13},{10,... | collective-permute-start | bytes 172040 | tf_op jit(solution)/shard_map/ppermute | solution.py:542
  14.7 0.0 collective-permute-start.6
  14.7 0.0 collective-permute-done.4.first
  14.7 2.5 %wave_step.1 = (f32[18,36,8,128]{3,2,1,0:T(8,128)}, f32[4,8,128]{2,1,0:T(8,128)S(1)}) custom-call(f32[18,36,8,128]{3,2,1,0:T(8,128)S(1)} %get-tuple-element.19.x, f32[16,8,128]{2,1,0:T(8,128)S(1)} %get-tuple-element.24.fields, f32[4,8,128]{2,1,0:T(8,128)S(1)} %get-tuple-element.29.coup, f32[16,128]{1,0:T(8,128)S(1)} %get-tuple-element.21.local, ...), custom_call_target="tpu_custom_call" | custom-call | flops 5971968 | bytes 5308416 | tf_op jit(solution)/shard_map/wave_step/pallas_call | solution.py:655
  17.2 0.5 %collective-permute-done.5.from_first = f32[112,128]{1,0:T(8,128)S(1)} collective-permute-done((f32[112,128]{1,0:T(8,128)S(1)}, f32[112,128]{1,0:T(8,128)S(1)}, u32[]{:S(2)}, u32[]{:S(2)}) %collective-permute-start.5) | collective-permute-done | bytes 57376 | tf_op jit(solution)/shard_map/ppermute | solution.py:542
  17.7 0.0 collective-permute-done.6.from_second
  17.7 1.1 %ocean_steps.1 = f32[2,4,8,128]{3,2,1,0:T(8,128)} custom-call(f32[112,128]{1,0:T(8,128)S(1)} %collective-permute-done.5.from_first, f32[112,128]{1,0:T(8,128)S(1)} %collective-permute-done.6.from_second, f32[16,8,128]{2,1,0:T(8,128)S(1)} %get-tuple-element.24.fields, f32[4,8,128]{2,1,0:T(8,128)S(1)} %get-tuple-element.34.coup, ...), custom_call_target="tpu_custom_call" | custom-call | flops 1048576 | bytes 1048576 | tf_op jit(solution)/shard_map/ocean_steps/pallas_call | solution.py:666
  (1 shorter events, 0.0 us)
Async XLA Ops:
  3.2 6.4 %collective-permute-start = (f32[176,128]{1,0:T(8,128)S(1)}, f32[176,128]{1,0:T(8,128)S(1)}, u32[]{:S(2)}, u32[]{:S(2)}) collective-permute-start(f32[176,128]{1,0:T(8,128)S(1)} %get-tuple-element.20.mine), channel_id=1, source_target_pairs={{0,16},{16,0},{1,17},{17,1},{2,18},{18,2},{3,19},{19,3},{4,20},{20... | collective-permute-start | bytes 270344 | tf_op jit(solution)/shard_map/ppermute | solution.py:529
  6.3 7.0 %collective-permute-start.3 = (f32[328,128]{1,0:T(8,128)S(1)}, f32[328,128]{1,0:T(8,128)S(1)}, u32[]{:S(2)}, u32[]{:S(2)}) collective-permute-start(f32[328,128]{1,0:T(8,128)S(1)} %pick_rows.2), channel_id=1, source_target_pairs={{0,1},{1,0},{2,3},{3,2},{4,8},{5,9},{6,10},{7,11},{8,4},{9,5},{10,... | collective-permute-start | bytes 503816 | tf_op jit(solution)/shard_map/ppermute | solution.py:542
  6.4 8.3 %collective-permute-start.4 = (f32[328,128]{1,0:T(8,128)S(1)}, f32[328,128]{1,0:T(8,128)S(1)}, u32[]{:S(2)}, u32[]{:S(2)}) collective-permute-start(f32[328,128]{1,0:T(8,128)S(1)} %pick_rows.3), channel_id=1, source_target_pairs={{0,4},{1,5},{2,6},{3,7},{4,0},{5,1},{6,2},{7,3},{8,12},{9,13},{10,... | collective-permute-start | bytes 503816 | tf_op jit(solution)/shard_map/ppermute | solution.py:542
  9.8 1.6 %collective-permute-start.1 = (f32[32,128]{1,0:T(8,128)S(1)}, f32[32,128]{1,0:T(8,128)S(1)}, u32[]{:S(2)}, u32[]{:S(2)}) collective-permute-start(f32[32,128]{1,0:T(8,128)S(1)} %get-tuple-element.25), channel_id=1, source_target_pairs={{0,3},{1,0},{2,1},{3,2},{4,7},{5,4},{6,5},{7,6},{8,11},{9,8},{10,9... | collective-permute-start | bytes 49160 | tf_op jit(solution)/shard_map/ppermute | solution.py:529
  10.0 3.3 %collective-permute-start.2 = (f32[32,128]{1,0:T(8,128)S(1)}, f32[32,128]{1,0:T(8,128)S(1)}, u32[]{:S(2)}, u32[]{:S(2)}) collective-permute-start(f32[32,128]{1,0:T(8,128)S(1)} %get-tuple-element.26), channel_id=1, source_target_pairs={{0,1},{1,2},{2,3},{3,0},{4,5},{5,6},{6,7},{7,4},{8,9},{9,10},{10,1... | collective-permute-start | bytes 49160 | tf_op jit(solution)/shard_map/ppermute | solution.py:529
  13.5 4.2 %collective-permute-start.5 = (f32[112,128]{1,0:T(8,128)S(1)}, f32[112,128]{1,0:T(8,128)S(1)}, u32[]{:S(2)}, u32[]{:S(2)}) collective-permute-start(f32[112,128]{1,0:T(8,128)S(1)} %get-tuple-element.32), channel_id=1, source_target_pairs={{0,4},{1,5},{2,6},{3,7},{4,0},{5,1},{6,2},{7,3},{8,12},{9,13},{10,... | collective-permute-start | bytes 172040 | tf_op jit(solution)/shard_map/ppermute | solution.py:542
  14.7 3.0 %collective-permute-start.6 = (f32[112,128]{1,0:T(8,128)S(1)}, f32[112,128]{1,0:T(8,128)S(1)}, u32[]{:S(2)}, u32[]{:S(2)}) collective-permute-start(f32[112,128]{1,0:T(8,128)S(1)} %get-tuple-element.33), channel_id=1, source_target_pairs={{0,1},{1,0},{2,3},{3,2},{4,8},{5,9},{6,10},{7,11},{8,4},{9,5},{10,... | collective-permute-start | bytes 172040 | tf_op jit(solution)/shard_map/ppermute | solution.py:542
